TPU v7x, 32 devices: a whole 2x2x4 slice. The times are simulated.
32 devices in a mesh: groups: 2 (over y), cells: 4 (over z), sect: 2 (over x), lev: 2 (over core).
Axes of the slice: x: 2, y: 2, z: 4, core: 2. Of those that a mesh axis runs over, the one named last changes fastest.
Arguments:
- spectrum: bfloat16 [1152, 32, 256], P(('cells', 'lev'), 'groups', 'sect'), parts along dimension 1, may hold values from -6 to 6
- courant_x: float32 [1152], P(('cells', 'lev')), may hold values from -0.45 to 0.45
- courant_y: float32 [1152], P(('cells', 'lev')), may hold values from -0.45 to 0.45
- growth: float32 [1152], replicated, may hold values from 0.5 to 2
- quartet: bfloat16 [1152, 1152], replicated, may hold values from -0.1875 to 0.1875
- coupler: bfloat16 [128, 1152], replicated, may hold values from -0.1875 to 0.1875
- atmosphere: float32 [64, 32, 256], P('lev', ('groups', 'cells'), 'sect'), parts along dimension 1, may hold values from -6 to 6
- ocean_state: float32 [64, 32, 256], P('lev', ('groups', 'cells'), 'sect'), parts along dimension 1, may hold values from -6 to 6
- sea_mask: int32 [32, 256], P(('groups', 'cells'), 'sect'), parts along dimension 0, may hold values 0 or 1
Outputs:
- spectrum_out: bfloat16 [1152, 32, 256], P(('cells', 'lev'), 'groups', 'sect'), parts along dimension 1
- atmosphere_out: float32 [64, 32, 256], P('lev', ('groups', 'cells'), 'sect'), parts along dimension 1
- ocean_out: float32 [64, 32, 256], P('lev', ('groups', 'cells'), 'sect'), parts along dimension 1
There are 2 independent parts, one for each index of `groups`. A program takes and returns all parts, laid end to end along the dimension named above; an argument that names none is the same for every part. Nothing has to cross between parts.
Inputs may be any that keep to these rules, and one draw needn't show every extreme that they name: `sea_mask`: 1 marks a sea cell, 0 a land cell.
All inputs are finite; a program needn't handle non-finite values. No bound on the sum of `sea_mask` on one device may be relied on, other than what follows from the above.
Results may differ from a plain program's by a relative error of at most 0.0062.
Values may be sent and summed in bfloat16 or wider, within the bound.
No kernel may reach another device: no remote copies, remote signals or barrier semaphores. Data moves between devices by JAX's collectives and lax.ppermute only.
A program may use at most 64 MiB of HBM per device.

v0:
```python
import functools

import jax
import jax.numpy as jnp
import numpy as np
from jax import lax
from jax.experimental import pallas as pl
from jax.experimental.pallas import tpu as pltpu
from jax.sharding import PartitionSpec as P

NSTEP = 2
LANES = 128
F32 = jnp.float32
BF16 = jnp.bfloat16
VMEM = pltpu.VMEM


def from_root(block, axis, source):
    block = jnp.where(lax.axis_index(axis) == source, block, jnp.zeros_like(block))
    return lax.psum(block, axis)


def extended_2(block, sides, width, periodic):
    for axis, dim in sides:
        count = lax.axis_size(axis)
        forward = [(i, i + 1) for i in range(count - 1)]
        if periodic:
            forward.append((count - 1, 0))
        backward = [(target, source) for source, target in forward]
        low = lax.ppermute(
            lax.slice_in_dim(block, block.shape[dim] - width, None, axis=dim), axis, forward
        )
        high = lax.ppermute(lax.slice_in_dim(block, 0, width, axis=dim), axis, backward)
        block = jnp.concatenate([low, block, high], axis=dim)
    return block


def upwind(values, courant, before, after):
    return jnp.maximum(courant, 0.0) * (values - before) + jnp.minimum(courant, 0.0) * (
        after - values
    )


def any_shape(
    spectrum, courant_x, courant_y, growth, quartet, coupler, atmosphere, ocean_state, sea_mask
):
    cell_tiles = lax.axis_size("cells")
    lev_parts = lax.axis_size("lev")
    blocks = cell_tiles * lev_parts
    comps_own, rows_all, row_width = spectrum.shape
    total_comps = comps_own * blocks
    cell_rows = rows_all // blocks
    level_count = coupler.shape[0] // 2
    row_start = lax.axis_index("lev") * cell_rows
    shift_x = courant_x[:, None, None]
    shift_y = courant_y[:, None, None]
    sea_rows = (
        lax.dynamic_slice_in_dim(sea_mask, row_start, cell_rows, 0)
        .astype(jnp.float32)
        .reshape(1, cell_rows * row_width)
    )
    growth_column = growth[:, None]
    forcing_sign = jnp.array([-0.3, 0.3], jnp.float32)[:, None, None, None]
    state = jnp.stack([atmosphere, ocean_state])
    energy = spectrum
    for counter in range(NSTEP):
        surface = from_root(state[:, 0], "lev", 0)
        surface_wind = surface[0] - surface[1]
        wind_rows = lax.dynamic_slice_in_dim(
            surface_wind * surface_wind, row_start, cell_rows, 0
        ).reshape(1, cell_rows * row_width)
        padded = extended_2(energy, (("sect", 2),), 1, True)
        values = padded[:, :, 1:-1].astype(jnp.float32)
        west_side = padded[:, :, :-2].astype(jnp.float32)
        east_side = padded[:, :, 2:].astype(jnp.float32)
        moved = values - upwind(values, shift_x, west_side, east_side)
        moved = moved - upwind(
            values, shift_y, jnp.roll(values, 1, axis=1), jnp.roll(values, -1, axis=1)
        )
        advected = moved.astype(jnp.bfloat16)
        pieces = advected.reshape(1, comps_own, blocks, cell_rows, row_width)
        on_cells = lax.all_to_all(pieces, ("cells", "lev"), split_axis=2, concat_axis=0, tiled=True)
        on_cells = on_cells.reshape(total_comps, cell_rows * row_width)
        cell_values = on_cells.astype(jnp.float32)
        paired = jnp.dot(quartet, on_cells, preferred_element_type=jnp.float32)
        squared = (cell_values * cell_values).astype(jnp.bfloat16)
        quad_square = jnp.dot(quartet, squared, preferred_element_type=jnp.float32)
        fresh = (
            cell_values
            + 0.3 * (cell_values * paired - quad_square)
            + 0.1 * growth_column * wind_rows
        ) / (1.0 + 0.1 * cell_values * cell_values)
        fresh = (fresh * sea_rows).astype(jnp.bfloat16)
        profile = jnp.dot(coupler, fresh, preferred_element_type=jnp.float32).reshape(
            2, level_count, cell_rows, row_width
        )
        forcing = lax.all_to_all(profile, "lev", split_axis=1, concat_axis=2, tiled=True)
        returned = fresh.reshape(blocks, comps_own, 1, cell_rows, row_width)
        returned = lax.all_to_all(
            returned, ("cells", "lev"), split_axis=0, concat_axis=2, tiled=True
        )
        energy = returned.reshape(comps_own, rows_all, row_width)
        extended = extended_2(state, (("lev", 1), ("cells", 2), ("sect", 3)), 1, False)
        state = relaxed(extended, 1) + forcing_sign * forcing
    return (energy, state[0], state[1])


def relaxed(extended, first):
    centre = (slice(None),) * first + (slice(1, -1),) * 3
    middle = extended[centre]

    def moved(dim, start):
        where = list(centre)
        where[first + dim] = slice(start, extended.shape[first + dim] - 2 + start)
        return extended[tuple(where)]

    lateral = moved(1, 2) + moved(1, 0) + moved(2, 2) + moved(2, 0) - 4.0 * middle
    upright = moved(0, 2) + moved(0, 0) - 2.0 * middle
    return middle + 0.1 * lateral + 0.1 * upright


def iota(shape, dim):
    return lax.broadcasted_iota(jnp.int32, shape, dim)


def over(values, unit):
    return values >> (unit.bit_length() - 1)


def within(values, unit):
    return values & (unit - 1)


def moved(values, matrix):
    return jnp.dot(values.astype(BF16), matrix, preferred_element_type=F32)


def split(values):
    head = values.astype(BF16).astype(F32)
    return head, values - head


def column_of(row, lanes):
    return jnp.transpose(jnp.broadcast_to(row, (lanes, row.shape[1])))


def swap_matrix(count, unit):
    index = np.arange(count * count * unit)
    a, b, i = index // (count * unit), index // unit % count, index % unit
    return index[:, None] == ((b * count + a) * unit + i)[None, :]


def neighbour_matrices(rows, width):
    cells = rows * width
    row, column = np.divmod(np.arange(cells), width)
    west = np.where(column > 0, row * width + column - 1, cells + row)
    east = np.where(
        column < width - 1, row * width + column + 1, cells + LANES - rows + row
    )
    north = (row - 1) % rows * width + column
    south = (row + 1) % rows * width + column
    source = np.arange(cells + LANES)[:, None]
    return np.concatenate([source == move[None, :] for move in (west, east, north, south)], axis=1)


def lateral_matrix(rows, width):
    cells = rows * width
    far_west, west, east, far_east = cells + LANES, cells, cells + LANES - rows, cells + 2 * LANES - rows
    place = {}
    for row in range(rows):
        for column in range(width):
            place[row, column] = row * width + column
        for column, start in ((-2, far_west), (-1, west), (width, east), (width + 1, far_east)):
            place[row, column] = start + row
    matrix = np.zeros((cells + 2 * LANES, cells + LANES), bool)
    for (row, column), target in place.items():
        if not -1 <= column <= width:
            continue
        for near in ((row - 1, column), (row + 1, column), (row, column - 1), (row, column + 1)):
            if near in place:
                matrix[place[near], target] = True
    return matrix


def edges_kernel(
    x_hbm, air_hbm, ocean_hbm, sea_hbm, courant_x_hbm, courant_y_hbm,
    by_row_ref, edge_ref, below_ref, state_ref, courant_x_ref, courant_y_ref,
    x_ref, air_ref, ocean_ref, sea_ref, wide, sems,
):
    comps, rows, columns = x_ref.shape
    levels, tile_rows, _ = air_ref.shape
    copies = [
        pltpu.make_async_copy(source, target, sems.at[index])
        for index, (source, target) in enumerate(
            (
                (x_hbm, x_ref),
                (air_hbm, air_ref),
                (ocean_hbm, ocean_ref),
                (sea_hbm, sea_ref),
                (courant_x_hbm, courant_x_ref),
                (courant_y_hbm, courant_y_ref),
            )
        )
    ]
    for copy in copies:
        copy.start()
    column, lane = iota((columns, LANES), 0), iota((columns, LANES), 1)

    block = within(over(lane, rows), 4)
    wanted = jnp.where(block < 2, columns - 2 + block, block - 2) == column
    row_of_lane = within(lane, rows)
    total = jnp.zeros((comps, LANES), F32)
    copies[0].wait()
    wide[...] = x_ref[...].astype(F32).reshape(comps * rows, columns)
    for row in range(rows):
        values = wide[pl.ds(row, comps, stride=rows), :].astype(BF16)
        by_row_ref[row] = values
        total += moved(values, (wanted & (row_of_lane == row)).astype(BF16))
    edge_ref[:comps] = total.astype(BF16)
    for copy in copies[1:]:
        copy.wait()
    owner = jnp.where(lax.axis_index("lev") == 0, 1.0, 0.0)
    head, tail = split((air_ref[0] - ocean_ref[0]) * owner)
    sea = sea_ref[...].astype(F32) * owner
    none = jnp.zeros_like(sea)
    edge_ref[comps : comps + 16] = jnp.concatenate([head, tail, sea, none], axis=0).astype(BF16)
    head, tail = split((air_ref[1] - ocean_ref[1]) * owner)
    below_ref[...] = jnp.concatenate([head, tail, none, none], axis=0).astype(BF16)

    values = [ref[:, row, :] for ref in (air_ref, ocean_ref) for row in range(tile_rows)]
    unit = columns // len(values)
    inner = within(lane, unit)
    wanted = (jnp.where(inner < 2, columns - 2 + inner, inner - 2) == column) & (inner < 4)
    total = jnp.zeros((levels, LANES), F32)
    for index, value in enumerate(values):
        value = value.astype(BF16)
        state_ref[:, index * columns : (index + 1) * columns] = value
        total += moved(value, (wanted & (over(lane, unit) == index)).astype(BF16))
    edge_ref[comps + 16 :] = total.astype(BF16)


def surface_rows(values, row_of_lane, tile_rows):
    first_row = lax.axis_index("cells") * tile_rows
    kept = row_of_lane == first_row + within(iota(values.shape, 0), tile_rows)
    kept = jnp.where(kept, values, 0.0).astype(BF16)
    target = iota((8, values.shape[0]), 0)
    source = over(iota((8, values.shape[0]), 1), tile_rows)
    source = jnp.where(source < 3, source, jnp.where(source < 4, 7, source - 1))
    adds = (target == jnp.where(source < 5, source, 7)).astype(BF16)
    return jnp.dot(adds, kept, preferred_element_type=F32)


def advect_kernel(
    groups, count, by_row_ref, edge_ref, below_ref, state_ref, courant_x_ref, courant_y_ref, swap_ref,
    packed_ref, cx_ref, cy_ref, gathered,
):
    rows, comps, columns = by_row_ref.shape
    levels = state_ref.shape[0]
    width = columns // count
    cells = rows * width
    cx_ref[...] = column_of(courant_x_ref[...], LANES)
    cy_ref[...] = column_of(courant_y_ref[...], LANES)
    source, target = iota((columns, 2 * columns), 0), iota((columns, 2 * columns), 1)
    step = jnp.where(target < columns, -1, 1)
    sides = (source == within(target + step, columns)).astype(BF16)
    for row in range(rows):
        here = by_row_ref[row].astype(F32)
        beside = moved(by_row_ref[row], sides)
        along = upwind(here, cx_ref[...], beside[:, :columns], beside[:, columns:])
        across = upwind(
            here,
            cy_ref[...],
            by_row_ref[row - 1 if row else rows - 1].astype(F32),
            by_row_ref[row + 1 if row < rows - 1 else 0].astype(F32),
        )
        tile, place = divmod(row, count)
        gathered[tile * comps : (tile + 1) * comps, place * columns : (place + 1) * columns] = (
            here - along - across
        ).astype(BF16)
    gathered[2 * comps :, :] = state_ref[...]
    for target in range(count // 2):
        lanes = slice(2 * target * LANES, 2 * (target + 1) * LANES)
        values = moved(gathered[...], swap_ref[:, lanes]).astype(BF16)
        for side in range(2):
            half = values[:, side * LANES : (side + 1) * LANES]
            packed_ref[2 * target + side, : 2 * comps, :] = half[: 2 * comps]
            start = 2 * comps + comps // groups + 16
            packed_ref[2 * target + side, start : start + levels, :] = half[2 * comps :]
    size = comps // groups

    own = iota((size, LANES), 1)
    riders = jnp.zeros((size, LANES), F32)
    for group in range(groups):
        span = slice(group * size, (group + 1) * size)
        for index, term in enumerate(split(cx_ref[span]) + split(cy_ref[span])):
            riders = jnp.where(own == 5 * rows + 4 * group + index, term, riders)

    values = jnp.concatenate([edge_ref[comps : comps + 16], below_ref[...]], axis=0)
    spot, lanes = iota((columns, count * cells), 0), iota((columns, count * cells), 1)
    repeat = spot == over(lanes, cells) * width + within(lanes, width)
    inland = moved(values, repeat.astype(BF16))
    inland = surface_rows(inland, over(within(iota(inland.shape, 1), cells), width), 4)
    spot, lanes = iota((columns, count * LANES), 0), iota((columns, count * LANES), 1)
    first = over(lanes, LANES) * width
    lanes = within(lanes, LANES)
    repeat = ((lanes < rows) & (spot == first - 1)) | (
        (lanes >= LANES - rows) & (spot == first + width)
    )
    shore = moved(values, repeat.astype(BF16))
    shore = surface_rows(shore, within(iota(shore.shape, 1), rows), 4)
    place = iota((8, LANES), 0)

    source, target_lane = iota((cells, 2 * LANES), 0), iota((cells, 2 * LANES), 1)
    block = over(within(target_lane, LANES), rows)
    row_start = within(target_lane, rows) * width
    ends = []
    for group in range(groups):
        west = (target_lane < LANES) & (block == 2 * group) & (source == row_start + width - 1)
        east = (target_lane >= LANES) & (block == (2 * group + 7) % 8) & (source == row_start)
        ends.append((west | east).astype(BF16))
    source, target_lane = iota((LANES, 2 * LANES), 0), iota((LANES, 2 * LANES), 1)
    inner = within(target_lane, width)
    back = (target_lane - inner) & (LANES - 1)
    shifts = []
    for start in (0, 8):
        west = (target_lane < LANES) & (inner >= start) & (inner < start + 2)
        west = west & (source == back + width - 2 + inner - start)
        east = (target_lane >= LANES) & (inner >= start + 2) & (inner < start + 4)
        east = east & (source == back + inner - start - 2)
        shifts.append((west | east).astype(BF16))
    beside, beside_state = [], []
    half = levels // 2
    for target in range(count):
        total = jnp.zeros((size, 2 * LANES), F32)
        for group in range(groups):
            for tile in range(2):
                span = slice(tile * comps + group * size, tile * comps + (group + 1) * size)
                rows_of = slice(tile * LANES, (tile + 1) * LANES)
                total += moved(packed_ref[target, span, :], ends[group][rows_of])
        beside.append(total)
        start = 2 * comps + size + 16
        low = moved(packed_ref[target, start : start + half, :], shifts[0])
        high = moved(packed_ref[target, start + half : start + levels, :], shifts[1])
        beside_state.append(low + high)
    for target in range(count):
        left, right = max(target - 1, 0), min(target + 1, count - 1)
        shared = riders + beside[left][:, :LANES] + beside[right][:, LANES:]
        packed_ref[target, 2 * comps : 2 * comps + size, :] = shared.astype(BF16)
        winds = [inland[:, (2 * target + i) * LANES : (2 * target + i + 1) * LANES] for i in range(2)]
        outer = pltpu.roll(shore[:, target * LANES : (target + 1) * LANES], 5, 0)
        winds[0] = jnp.where(place < 5, winds[0], outer)
        start = 2 * comps + size
        packed_ref[target, start : start + 16, :] = jnp.concatenate(winds, axis=0).astype(BF16)
        start += 16 + levels
        outer = beside_state[left][:, :LANES] + beside_state[right][:, LANES:]
        packed_ref[target, start : start + half, :] = outer.astype(BF16)


def coast_kernel(groups, count, rows, packed_ref, edge_ref, halo_ref, cx_ref, cy_ref, *out_refs):
    comps = cx_ref.shape[0]
    size = comps // groups
    levels = halo_ref.shape[0] - comps - 16
    cells = 2 * LANES
    width = cells // rows
    half = levels // 2
    block = over(iota((comps, LANES), 1), rows)
    near = jnp.where((block < 2) | (block >= 6), halo_ref[:comps], edge_ref[:comps])
    source, target = iota((LANES, 4 * LANES), 0), iota((LANES, 4 * LANES), 1)
    lane = within(target, LANES)
    row = within(lane, rows)
    kind = over(target, LANES)
    shift = jnp.where(
        kind == 0,
        within(lane - rows, LANES),
        jnp.where(
            kind == 1,
            within(lane + rows, LANES),
            lane - row + within(row + jnp.where(kind == 2, -1, 1), rows),
        ),
    )
    four = moved(near, (source == shift).astype(BF16))
    near = near.astype(F32)
    near = (
        near
        - upwind(near, cx_ref[...], four[:, :LANES], four[:, LANES : 2 * LANES])
        - upwind(near, cy_ref[...], four[:, 2 * LANES : 3 * LANES], four[:, 3 * LANES :])
    )
    source, target = iota((LANES, cells), 0), iota((LANES, cells), 1)
    column, row = within(target, width), over(target, width)
    spread = ((column == 0) & (source == 2 * rows + row)) | (
        (column == width - 1) & (source == 5 * rows + row)
    )
    ends = moved(near, spread.astype(BF16))
    shared = jnp.zeros((size, LANES), F32)
    source, target = iota((LANES, LANES), 0), iota((LANES, LANES), 1)
    for group in range(groups):
        there = over(target, rows)
        from_block = jnp.where(
            there == 2 * group, 1, jnp.where(there == (2 * group + 7) % 8, 6, LANES)
        )
        spread = source == from_block * rows + within(target, rows)
        shared += moved(near[group * size : (group + 1) * size], spread.astype(BF16))
    repeat = ((target < rows) & (source == LANES - 1)) | ((target >= LANES - rows) & (source == 0))
    coast = moved(halo_ref[comps : comps + 16], repeat.astype(BF16))
    coast = jnp.concatenate([coast, jnp.zeros_like(coast)], axis=0)
    coast = surface_rows(coast, within(iota(coast.shape, 1), rows), 4)
    coast = pltpu.roll(coast, 5, 0)
    coast = jnp.concatenate([coast, jnp.zeros_like(coast)], axis=0)
    inner = within(target, width)
    low = (source == target) & (inner < 4)
    high = (source == target - 8) & (inner >= 8) & (inner < 12)
    state = moved(halo_ref[comps + 16 : comps + 16 + half], low.astype(BF16))
    state += moved(halo_ref[comps + 16 + half :], high.astype(BF16))
    me = lax.axis_index(("cells", "lev"))
    for slot in range(count):
        target = lax.rem(me + slot, count)
        out_refs[slot][...] = packed_ref[target]
        place, lane = iota((16, LANES), 0), iota((16, LANES), 1)
        outer = (place >= 5) & (place < 8)

        def patch(start, stop, where, values):
            old = out_refs[slot][start:stop].astype(F32)
            out_refs[slot][start:stop] = jnp.where(where, values, old).astype(BF16)

        def patch_ends(east):
            column = within(iota((comps, LANES), 1), width)
            for tile in range(2):
                values = ends[:, tile * LANES : (tile + 1) * LANES]
                where = column == (width - 1 if east else 0)
                patch(tile * comps, (tile + 1) * comps, where, values)
            own = over(iota((size, LANES), 1), rows)
            where = own < 0
            for group in range(groups):
                where = where | (own == ((2 * group + 7) % 8 if east else 2 * group))
            patch(2 * comps, 2 * comps + size, where, shared)
            start = 2 * comps + size
            side = lane >= LANES - rows if east else lane < rows
            patch(start, start + 16, outer & side, coast)
            start += 16 + levels
            inner = within(iota((half, LANES), 1), 8)
            patch(start, start + half, (inner >= 2) == east, state)

        @pl.when(target == 0)
        def _():
            patch_ends(False)

        @pl.when(target == count - 1)
        def _():
            patch_ends(True)


def steps_kernel(
    groups, count, rows, quartet_ref, coupler_ref, growth_ref, beside_ref, lateral_ref, *refs
):
    in_refs, refs = refs[:count], refs[count:]
    out_refs, refs = refs[:count], refs[count:]
    first_in, fresh, second_in, last, shares, factors, state, ends = refs
    total = quartet_ref.shape[0]
    comps = total // count
    size = comps // groups
    cells = 2 * LANES
    wide = 3 * LANES
    width = cells // rows
    levels = coupler_ref.shape[0] // 2
    half = shares.shape[1]
    me = lax.axis_index(("cells", "lev"))
    west_end = (me == 0) & (lax.axis_index("sect") == 0)
    east_end = (me == count - 1) & (lax.axis_index("sect") == lax.axis_size("sect") - 1)
    factors[:, 8:16] = column_of(0.1 * growth_ref[...], 8)

    source, target = iota((LANES, 2 * LANES), 0), iota((LANES, 2 * LANES), 1)
    block = over(target, rows)
    opened = []
    for group in range(groups):
        from_block = jnp.where(
            block == 0, 2 * group, jnp.where(block == 7, (2 * group + 7) % 8, LANES)
        )
        column = source == from_block * rows + within(target, rows)
        rider = source - (5 * rows + 4 * group)
        rider = (rider >= 0) & (rider < 4) & (over(rider, 2) == target - LANES)
        opened.append((column | rider).astype(BF16))
    winds = jnp.zeros((16, LANES), F32)
    for slot in range(count):
        source = lax.rem(me - slot + count, count)
        start = pl.multiple_of(source * comps, 16)
        span = pl.ds(start, comps)
        for tile in range(2):
            values = in_refs[slot][tile * comps : (tile + 1) * comps]
            first_in[span, tile * LANES : (tile + 1) * LANES] = values
            values = values.astype(F32)
            first_in[span, wide + tile * LANES : wide + (tile + 1) * LANES] = (
                values * values
            ).astype(BF16)
        for group in range(groups):
            span = pl.ds(pl.multiple_of(start + group * size, 16), size)
            values = moved(in_refs[slot][2 * comps : 2 * comps + size], opened[group])
            first_in[span, cells:wide] = values[:, :LANES].astype(BF16)
            values_8 = values[:, LANES : LANES + 8]
            values = values[:, :LANES]
            first_in[span, wide + cells :] = (values * values).astype(BF16)
            factors[span, :8] = values_8
        place = 2 * comps + size
        winds += in_refs[slot][place : place + 16].astype(F32)
        place += 16
        state[source] = in_refs[slot][place : place + half]
        ends[source] = in_refs[slot][place + half :]

    first, second = winds[:8], winds[8:]
    outer = pltpu.roll(first, 3, 0)

    def joined(tile):
        return tile[:1] + tile[1:2]

    surface = jnp.concatenate([joined(first), joined(second), joined(outer)], axis=1)
    terms = jnp.concatenate([first, second, outer], axis=1)
    sea = terms[2:3]
    below = jnp.concatenate([joined(first[3:5]), joined(second[3:5])], axis=1)
    wind = surface * surface

    def renew(values, products, growth, wind, sea):
        half = values.shape[1]
        paired, quad_square = products[:, :half], products[:, half:]
        below = 1.0 + 0.1 * values * values
        inverse = pl.reciprocal(below, approx=True)
        inverse = inverse * (2.0 - below * inverse)
        return (values + 0.3 * (values * paired - quad_square) + growth * wind) * inverse * sea

    part = total // 2
    for step in range(2):
        span = slice(step * part, (step + 1) * part)
        products = jnp.dot(quartet_ref[span, :], first_in[...], preferred_element_type=F32)
        values = first_in[span, :wide].astype(F32)
        fresh[span, :] = renew(values, products, factors[span, 8:9], wind, sea).astype(BF16)
    part = total // 8
    for step in range(8):
        span = slice(step * part, (step + 1) * part)
        beside = jnp.dot(fresh[span, :], beside_ref[...], preferred_element_type=F32)
        here = fresh[span, :cells].astype(F32)
        cx = jnp.broadcast_to(factors[span, 0:1], here.shape)
        cy = jnp.broadcast_to(factors[span, 1:2], here.shape)
        values = (
            here
            - upwind(here, cx, beside[:, :cells], beside[:, cells : 2 * cells])
            - upwind(here, cy, beside[:, 2 * cells : 3 * cells], beside[:, 3 * cells :])
        ).astype(BF16)
        second_in[span, :cells] = values
        values = values.astype(F32)
        second_in[span, cells:] = (values * values).astype(BF16)

    lev_parts = levels // half
    halves = iota((half, LANES), 1) < LANES // 2

    def collected(values):
        fields = []
        for kind in range(2):
            for part in range(lev_parts):
                tiles = []
                for pair in range(count // lev_parts // 2):
                    left = values[2 * pair * lev_parts + part].astype(F32)
                    right = values[(2 * pair + 1) * lev_parts + part].astype(F32)
                    if kind == 0:
                        right = pltpu.roll(right, LANES // 2, 1)
                    else:
                        left = pltpu.roll(left, LANES // 2, 1)
                    tiles.append(jnp.where(halves[: left.shape[0]], left, right))
                fields.append(jnp.concatenate(tiles, axis=1))
        return fields

    inner = jnp.concatenate(collected(state), axis=0)
    source, target = iota((cells, cells), 0), iota((cells, cells), 1)
    far = over(target, LANES)
    block = over(within(target, LANES), rows)
    order = jnp.where(block == 0, jnp.where(far == 0, 1, 0), jnp.where(far == 0, 2, 3))
    used = (block == 0) | (block == 7)
    spread = [
        ((source == within(target, rows) * width + order + 8 * high) & used).astype(BF16)
        for high in range(2)
    ]
    outer = []
    for field in collected(ends):
        outer += [moved(field, spread[0]), moved(field, spread[1])]
    outer = jnp.concatenate(outer, axis=0)

    def bounded(values):
        lane = iota(values.shape, 1)
        outside = (west_end & (lane < rows)) | (east_end & (lane >= LANES - rows))
        return jnp.where(outside, 0.0, values)

    outer = [bounded(outer[:, :LANES]), bounded(outer[:, LANES:])]

    def relaxed_once(here, lateral):
        level = within(iota(here.shape, 0), levels)
        lateral = lateral - 4.0 * here
        above = jnp.where(level == 0, 0.0, pltpu.roll(here, 1, 0))
        under = jnp.where(level == levels - 1, 0.0, pltpu.roll(here, 2 * levels - 1, 0))
        return here + 0.1 * lateral + 0.1 * (above + under - 2.0 * here)

    sign = jnp.where(iota((2 * levels, 1), 0) < levels, -0.3, 0.3)
    forced = jnp.dot(coupler_ref[...], fresh[...], preferred_element_type=F32) * sign
    here = jnp.concatenate([inner] + outer, axis=1)
    fields = relaxed_once(here[:, :wide], moved(here, lateral_ref[...])) + forced
    fields = jnp.concatenate([fields[:, :cells], bounded(fields[:, cells:])], axis=1)
    near = lateral_ref[:wide, :cells]
    head, tail = split(fields)
    fields = relaxed_once(fields[:, :cells], moved(head, near) + moved(tail, near))

    terms = jnp.concatenate([terms[:, :cells], bounded(terms[:, cells:])], axis=1)
    lateral = joined(moved(terms, near))
    calm = surface[:, :cells]
    calm = calm + 0.1 * (lateral - 4.0 * calm) + 0.1 * (below - 2.0 * calm)
    later = calm + forced[:1, :cells] - forced[levels : levels + 1, :cells]
    later = later * later

    part = total // 2
    for step in range(2):
        span = slice(step * part, (step + 1) * part)
        products = jnp.dot(quartet_ref[span, :], second_in[...], preferred_element_type=F32)
        values = second_in[span, :cells].astype(F32)
        done = renew(values, products, factors[span, 8:9], later, sea[:, :cells])
        last[span, :] = done.astype(BF16)

    forced = jnp.dot(coupler_ref[...], last[...], preferred_element_type=F32)
    carried = fields + sign * forced
    for target in range(count):
        cell_tile, lev_part = target // lev_parts, target % lev_parts
        columns = slice((cell_tile // 2) * LANES, (cell_tile // 2 + 1) * LANES)
        air = carried[lev_part * half : (lev_part + 1) * half, columns]
        sea_part = carried[levels + lev_part * half : levels + (lev_part + 1) * half, columns]
        if cell_tile % 2:
            air = pltpu.roll(air, LANES // 2, 1)
        else:
            sea_part = pltpu.roll(sea_part, LANES // 2, 1)
        shares[target] = jnp.where(halves, air, sea_part).astype(BF16)
    for slot in range(count):
        target = lax.rem(me + slot, count)
        span = pl.ds(pl.multiple_of(target * comps, 16), comps)
        out_refs[slot][:comps] = last[span, :LANES]
        out_refs[slot][comps : 2 * comps] = last[span, LANES:]
        out_refs[slot][2 * comps :] = shares[target]


def finish_kernel(count, swap_ref, *refs):
    in_refs, refs = refs[:count], refs[count:]
    energy_ref, air_ref, ocean_ref, gathered, wide, narrow = refs
    comps, rows, columns = energy_ref.shape
    levels, tile_rows, _ = air_ref.shape
    me = lax.axis_index(("cells", "lev"))
    for slot in range(count):
        source = lax.rem(me - slot + count, count)
        gathered[:, pl.ds(pl.multiple_of(source * columns, columns), columns)] = in_refs[slot][...]
    for pair in range(count // 2):
        lanes = slice(2 * pair * columns, 2 * (pair + 1) * columns)
        values = moved(gathered[...], swap_ref[:, lanes])
        for side in range(2):
            index = 2 * pair + side
            part = values[:, side * columns : (side + 1) * columns]
            for tile in range(rows // count):
                wide[pl.ds(tile * count + index, comps, stride=rows), :] = part[
                    tile * comps : (tile + 1) * comps
                ]
            kind, row = divmod(index, tile_rows)
            narrow[pl.ds(kind * levels * tile_rows + row, levels, stride=tile_rows), :] = part[
                2 * comps :
            ]
    energy_ref[...] = wide[...].reshape(comps, rows, columns).astype(energy_ref.dtype)
    size = levels * tile_rows
    air_ref[...] = narrow[:size, :].reshape(air_ref.shape)
    ocean_ref[...] = narrow[size:, :].reshape(ocean_ref.shape)


def spread_out(pieces, axes, count):
    received = [pieces[0]]
    for shift in range(1, count):
        pairs = [(index, (index + shift) % count) for index in range(count)]
        received.append(lax.ppermute(pieces[shift], axes, pairs))
    return received


def by_columns(
    spectrum, courant_x, courant_y, growth, quartet, coupler, atmosphere, ocean_state, sea_mask
):
    axes = ("cells", "lev")
    count = lax.axis_size("cells") * lax.axis_size("lev")
    sects = lax.axis_size("sect")
    comps, rows, columns = spectrum.shape
    total = comps * count
    width = columns // count
    cells = rows * width
    levels_own, tile_rows, _ = atmosphere.shape
    groups = 3 if comps % 48 == 0 else 2
    whole = pl.BlockSpec(memory_space=VMEM)
    far = pl.BlockSpec(memory_space=pltpu.HBM)

    def shape(*dims, kind=BF16):
        return jax.ShapeDtypeStruct(dims, kind)

    def call(kernel, outs, *args, kept=(), specs=None, flops=0, mega=16):
        return pl.pallas_call(
            kernel,
            out_shape=outs,
            in_specs=specs or [whole] * len(args),
            out_specs=jax.tree.map(lambda _: whole, outs),
            scratch_shapes=list(kept),
            compiler_params=pltpu.CompilerParams(vmem_limit_bytes=mega * 1024 * 1024),
            cost_estimate=pl.CostEstimate(flops=flops, bytes_accessed=4000000, transcendentals=0),
        )(*args)

    swap = jnp.asarray(swap_matrix(count, width), BF16)
    row = shape(1, comps, kind=F32)
    by_row, edge, below, state, row_x, row_y = call(
        edges_kernel,
        (
            shape(rows, comps, columns),
            shape(comps + 16 + levels_own, LANES),
            shape(16, LANES),
            shape(levels_own, count * columns),
            row,
            row,
        ),
        spectrum,
        atmosphere,
        ocean_state,
        sea_mask,
        courant_x[None],
        courant_y[None],
        specs=[far] * 6,
        kept=[
            VMEM(spectrum.shape, BF16),
            VMEM(atmosphere.shape, F32),
            VMEM(ocean_state.shape, F32),
            VMEM(sea_mask.shape, sea_mask.dtype),
            VMEM((comps * rows, columns), F32),
            pltpu.SemaphoreType.DMA((6,)),
        ],
    )
    halo = lax.ppermute(edge, "sect", [(0, 1), (1, 0)])

    size = 2 * comps + comps // groups + 16 + levels_own + levels_own // 2
    factor = shape(comps, LANES, kind=F32)
    packed, factor_x, factor_y = call(
        functools.partial(advect_kernel, groups, count),
        (shape(count, size, LANES), factor, factor),
        by_row,
        edge,
        below,
        state,
        row_x,
        row_y,
        swap,
        kept=[VMEM((2 * comps + levels_own, count * columns), BF16)],
        flops=2000000000,
    )
    pieces = call(
        functools.partial(coast_kernel, groups, count, rows),
        (shape(size, LANES),) * count,
        packed,
        edge,
        halo,
        factor_x,
        factor_y,
    )
    received = spread_out(pieces, axes, count)

    results = call(
        functools.partial(steps_kernel, groups, count, rows),
        (shape(2 * comps + levels_own, LANES),) * count,
        quartet,
        coupler,
        growth[None],
        jnp.asarray(neighbour_matrices(rows, width), BF16),
        jnp.asarray(lateral_matrix(rows, width), BF16),
        *received,
        kept=[
            VMEM((total, 6 * LANES), BF16),
            VMEM((total, 3 * LANES), BF16),
            VMEM((total, 4 * LANES), BF16),
            VMEM((total, cells), BF16),
            VMEM((count, levels_own, LANES), BF16),
            VMEM((total, LANES), F32),
            VMEM((count, levels_own, LANES), BF16),
            VMEM((count, levels_own // 2, LANES), BF16),
        ],
        mega=32,
    )
    returned = spread_out(results, axes, count)

    return call(
        functools.partial(finish_kernel, count),
        (
            shape(*spectrum.shape),
            shape(*atmosphere.shape, kind=F32),
            shape(*ocean_state.shape, kind=F32),
        ),
        swap,
        *returned,
        kept=[
            VMEM((2 * comps + levels_own, count * columns), BF16),
            VMEM((comps * rows, columns), F32),
            VMEM((2 * levels_own * tile_rows, columns), F32),
        ],
    )


def on_device(spectrum, *rest):
    atmosphere = rest[5]
    blocks = lax.axis_size("cells") * lax.axis_size("lev")
    comps, rows, columns = spectrum.shape
    fits = (
        columns == LANES
        and blocks == 8
        and lax.axis_size("sect") == 2
        and rows * (columns // blocks) == 2 * LANES
        and atmosphere.shape[1] * (columns // blocks) * 2 == LANES
        and any(comps % (16 * groups) == 0 for groups in (3, 2))
        and atmosphere.shape[0] % 16 == 0
        and NSTEP == 2
    )
    return (by_columns if fits else any_shape)(spectrum, *rest)


def solution(mesh):
    in_specs = (
        P(("cells", "lev"), "groups", "sect"),
        P(("cells", "lev")),
        P(("cells", "lev")),
        P(),
        P(),
        P(),
        P("lev", ("groups", "cells"), "sect"),
        P("lev", ("groups", "cells"), "sect"),
        P(("groups", "cells"), "sect"),
    )
    out_specs = (
        P(("cells", "lev"), "groups", "sect"),
        P("lev", ("groups", "cells"), "sect"),
        P("lev", ("groups", "cells"), "sect"),
    )
    return jax.shard_map(
        on_device, mesh=mesh, in_specs=in_specs, out_specs=out_specs, check_vma=False
    )
```

profile of v0, /device:TPU:0, one launch (start us, length us, event | category | flops | bytes accessed | tf_op | source)
XLA Modules:
  0.0 63.9 jit_solution(14587810794185520334)
XLA Ops:
  0.6 1.1 %copy-done.4 = bf16[144,16,128]{2,1,0:T(8,128)(2,1)S(1)} copy-done((bf16[144,16,128]{2,1,0:T(8,128)(2,1)S(1)}, bf16[144,16,128]{2,1,0:T(8,128)(2,1)}, u32[]{:S(2)}) %copy-start.4) | copy-done | bytes 589848
  1.7 0.8 %copy-done.7 = f32[32,4,128]{2,1,0:T(4,128)S(1)} copy-done((f32[32,4,128]{2,1,0:T(4,128)S(1)}, f32[32,4,128]{2,1,0:T(4,128)}, u32[]{:S(2)}) %copy-start.7) | copy-done | bytes 65560
  2.5 0.8 %copy-done.8 = f32[32,4,128]{2,1,0:T(4,128)S(1)} copy-done((f32[32,4,128]{2,1,0:T(4,128)S(1)}, f32[32,4,128]{2,1,0:T(4,128)}, u32[]{:S(2)}) %copy-start.8) | copy-done | bytes 65560
  3.4 0.7 %copy-done.9 = s32[4,128]{1,0:T(4,128)S(1)} copy-done((s32[4,128]{1,0:T(4,128)S(1)}, s32[4,128]{1,0:T(4,128)}, u32[]{:S(2)}) %copy-start.9) | copy-done | bytes 2072
  4.1 0.7 %copy-done.10 = f32[144]{0:T(256)S(1)} copy-done((f32[144]{0:T(256)S(1)}, f32[144]{0:T(256)}, u32[]{:S(2)}) %copy-start.10) | copy-done | bytes 600
  4.7 0.7 %copy-done.11 = f32[144]{0:T(256)S(1)} copy-done((f32[144]{0:T(256)S(1)}, f32[144]{0:T(256)}, u32[]{:S(2)}) %copy-start.11) | copy-done | bytes 600
  5.4 1.2 %shard_map.139 = (bf16[16,144,128]{2,1,0:T(8,128)(2,1)S(1)}, bf16[192,128]{1,0:T(8,128)(2,1)S(1)}, bf16[16,128]{1,0:T(8,128)(2,1)S(1)}, bf16[32,1024]{1,0:T(8,12...) custom-call(bf16[144,16,128]{2,1,0:T(8,128)(2,1)S(1)} %copy-done.4, f32[32,4,128]{2,1,0:T(4,128)S(1)} %copy-done.7, ...), custom_call_target="tpu_custom_call" | custom-call | bytes 4000000 | tf_op jit(solution)/shard_map/pallas_call | solution.py:698
  6.7 3.0 %collective-permute-start = (bf16[192,128]{1,0:T(8,128)(2,1)S(1)}, bf16[192,128]{1,0:T(8,128)(2,1)S(1)}, u32[]{:S(2)}, u32[]{:S(2)}) collective-permute-start(bf16[192,128]{1,0:T(8,128)(2,1)S(1)} %get-tuple-element.29.edge_ref), channel_id=1, source_target_pairs={{0,2},{2,0},{1,3},{3,1},{4,6},{6,4},{5,7},{7,5},{8,10},{10,8},{9,1... | collective-permute-start | bytes 147464 | tf_op jit(solution)/shard_map/ppermute | solution.py:736
  9.7 1.6 %copy-done.1 = bf16[1024,1024]{1,0:T(8,128)(2,1)S(1)} copy-done((bf16[1024,1024]{1,0:T(8,128)(2,1)S(1)}, bf16[1024,1024]{1,0:T(8,128)(2,1)}, u32[]{:S(2)}) %copy-start.1) | copy-done | bytes 2097176
  11.3 2.7 %shard_map.140 = (bf16[8,400,128]{2,1,0:T(8,128)(2,1)S(1)}, f32[144,128]{1,0:T(8,128)S(1)}, f32[144,128]{1,0:T(8,128)S(1)}) custom-call(bf16[16,144,128]{2,1,0:T(8,128)(2,1)S(1)} %get-tuple-element.28.by_row_ref, bf16[192,128]{1,0:T(8,128)(2,1)S(1)} %get-tuple-element.29.edge_ref, bf16[16,128]{1,0:T(8,128)(2,1)S(1)} %get-tuple-element.30.below_ref, ...), custom_call_target="tpu_custom_call" | custom-call | flops 2000000000 | bytes 4000000 | tf_op jit(solution)/shard_map/pallas_call | solution.py:698
  14.0 0.6 %shard_map.141 = (bf16[400,128]{1,0:T(8,128)(2,1)S(1)}, bf16[400,128]{1,0:T(8,128)(2,1)S(1)}, bf16[400,128]{1,0:T(8,128)(2,1)S(1)}, bf16[400,128]{1,0:T(8,128)(2...) custom-call(bf16[8,400,128]{2,1,0:T(8,128)(2,1)S(1)} %get-tuple-elem, ...), custom_call_target="tpu_custom_call" | custom-call | bytes 4000000 | tf_op jit(solution)/shard_map/pallas_call | solution.py:698
  14.6 0.0 copy-start.2
  14.6 0.1 collective-permute-start.1
  14.7 1.6 %collective-permute-start.2 = (bf16[400,128]{1,0:T(8,128)(2,1)S(1)}, bf16[400,128]{1,0:T(8,128)(2,1)S(1)}, u32[]{:S(2)}, u32[]{:S(2)}) collective-permute-start(bf16[400,128]{1,0:T(8,128)(2,1)S(1)} %get-tuple-element.39), channel_id=1, source_target_pairs={{0,4},{1,5},{4,8},{5,9},{8,12},{9,13},{12,0},{13,1},{2,6},{3,7},{6... | collective-permute-start | bytes 307208 | tf_op jit(solution)/shard_map/ppermute | solution.py:675
  16.3 2.5 %collective-permute-start.3 = (bf16[400,128]{1,0:T(8,128)(2,1)S(1)}, bf16[400,128]{1,0:T(8,128)(2,1)S(1)}, u32[]{:S(2)}, u32[]{:S(2)}) collective-permute-start(bf16[400,128]{1,0:T(8,128)(2,1)S(1)} %get-tuple-element.40), channel_id=1, source_target_pairs={{0,5},{1,8},{4,9},{5,12},{8,13},{9,0},{12,1},{13,4},{2,7},{3,10},{... | collective-permute-start | bytes 307208 | tf_op jit(solution)/shard_map/ppermute | solution.py:675
  18.8 1.2 %collective-permute-start.4 = (bf16[400,128]{1,0:T(8,128)(2,1)S(1)}, bf16[400,128]{1,0:T(8,128)(2,1)S(1)}, u32[]{:S(2)}, u32[]{:S(2)}) collective-permute-start(bf16[400,128]{1,0:T(8,128)(2,1)S(1)} %get-tuple-element.41), channel_id=1, source_target_pairs={{0,8},{1,9},{4,12},{5,13},{8,0},{9,1},{12,4},{13,5},{2,10},{3,11},... | collective-permute-start | bytes 307208 | tf_op jit(solution)/shard_map/ppermute | solution.py:675
  20.1 1.2 %collective-permute-start.5 = (bf16[400,128]{1,0:T(8,128)(2,1)S(1)}, bf16[400,128]{1,0:T(8,128)(2,1)S(1)}, u32[]{:S(2)}, u32[]{:S(2)}) collective-permute-start(bf16[400,128]{1,0:T(8,128)(2,1)S(1)} %get-tuple-element.42), channel_id=1, source_target_pairs={{0,9},{1,12},{4,13},{5,0},{8,1},{9,4},{12,5},{13,8},{2,11},{3,14},... | collective-permute-start | bytes 307208 | tf_op jit(solution)/shard_map/ppermute | solution.py:675
  21.3 1.6 %collective-permute-start.6 = (bf16[400,128]{1,0:T(8,128)(2,1)S(1)}, bf16[400,128]{1,0:T(8,128)(2,1)S(1)}, u32[]{:S(2)}, u32[]{:S(2)}) collective-permute-start(bf16[400,128]{1,0:T(8,128)(2,1)S(1)} %get-tuple-element.43), channel_id=1, source_target_pairs={{0,12},{1,13},{4,0},{5,1},{8,4},{9,5},{12,8},{13,9},{2,14},{3,15},... | collective-permute-start | bytes 307208 | tf_op jit(solution)/shard_map/ppermute | solution.py:675
  22.9 1.6 %collective-permute-start.7 = (bf16[400,128]{1,0:T(8,128)(2,1)S(1)}, bf16[400,128]{1,0:T(8,128)(2,1)S(1)}, u32[]{:S(2)}, u32[]{:S(2)}) collective-permute-start(bf16[400,128]{1,0:T(8,128)(2,1)S(1)} %get-tuple-element.44), channel_id=1, source_target_pairs={{0,13},{1,0},{4,1},{5,4},{8,5},{9,8},{12,9},{13,12},{2,15},{3,2},{... | collective-permute-start | bytes 307208 | tf_op jit(solution)/shard_map/ppermute | solution.py:675
  24.5 5.9 %collective-permute-done.3.refs_3_ = bf16[400,128]{1,0:T(8,128)(2,1)S(1)} collective-permute-done((bf16[400,128]{1,0:T(8,128)(2,1)S(1)}, bf16[400,128]{1,0:T(8,128)(2,1)S(1)}, u32[]{:S(2)}, u32[]{:S(2)}) %collective-permute-start.3) | collective-permute-done | bytes 102432 | tf_op jit(solution)/shard_map/ppermute | solution.py:675
  30.4 0.2 collective-permute-done.4.refs_4_
  30.6 7.8 %shard_map.142 = (bf16[320,128]{1,0:T(8,128)(2,1)S(1)}, bf16[320,128]{1,0:T(8,128)(2,1)S(1)}, bf16[320,128]{1,0:T(8,128)(2,1)S(1)}, bf16[320,128]{1,0:T(8,128)(2...) custom-call(bf16[1152,1152]{1,0:T(8,128)(2,1)S(1)} %copy-done, ...), custom_call_target="tpu_custom_call" | custom-call | bytes 4000000 | tf_op jit(solution)/shard_map/pallas_call | solution.py:698
  38.4 6.4 %collective-permute-start.10 = (bf16[320,128]{1,0:T(8,128)(2,1)S(1)}, bf16[320,128]{1,0:T(8,128)(2,1)S(1)}, u32[]{:S(2)}, u32[]{:S(2)}) collective-permute-start(bf16[320,128]{1,0:T(8,128)(2,1)S(1)} %get-tuple-element.48), channel_id=1, source_target_pairs={{0,5},{1,8},{4,9},{5,12},{8,13},{9,0},{12,1},{13,4},{2,7},{3,10},{... | collective-permute-start | bytes 245768 | tf_op jit(solution)/shard_map/ppermute | solution.py:675
  44.9 1.7 %collective-permute-start.11 = (bf16[320,128]{1,0:T(8,128)(2,1)S(1)}, bf16[320,128]{1,0:T(8,128)(2,1)S(1)}, u32[]{:S(2)}, u32[]{:S(2)}) collective-permute-start(bf16[320,128]{1,0:T(8,128)(2,1)S(1)} %get-tuple-element.49), channel_id=1, source_target_pairs={{0,8},{1,9},{4,12},{5,13},{8,0},{9,1},{12,4},{13,5},{2,10},{3,11},... | collective-permute-start | bytes 245768 | tf_op jit(solution)/shard_map/ppermute | solution.py:675
  46.6 0.2 collective-permute-start.12
  46.8 2.0 %collective-permute-start.13 = (bf16[320,128]{1,0:T(8,128)(2,1)S(1)}, bf16[320,128]{1,0:T(8,128)(2,1)S(1)}, u32[]{:S(2)}, u32[]{:S(2)}) collective-permute-start(bf16[320,128]{1,0:T(8,128)(2,1)S(1)} %get-tuple-element.51), channel_id=1, source_target_pairs={{0,12},{1,13},{4,0},{5,1},{8,4},{9,5},{12,8},{13,9},{2,14},{3,15},... | collective-permute-start | bytes 245768 | tf_op jit(solution)/shard_map/ppermute | solution.py:675
  48.7 0.3 collective-permute-start.14
  49.0 0.2 collective-permute-start.8
  49.3 3.6 %collective-permute-done.11.refs_4_ = bf16[320,128]{1,0:T(8,128)(2,1)S(1)} collective-permute-done((bf16[320,128]{1,0:T(8,128)(2,1)S(1)}, bf16[320,128]{1,0:T(8,128)(2,1)S(1)}, u32[]{:S(2)}, u32[]{:S(2)}) %collective-permute-start.11) | collective-permute-done | bytes 81952 | tf_op jit(solution)/shard_map/ppermute | solution.py:675
  52.9 2.9 %collective-permute-start.9 = (bf16[320,128]{1,0:T(8,128)(2,1)S(1)}, bf16[320,128]{1,0:T(8,128)(2,1)S(1)}, u32[]{:S(2)}, u32[]{:S(2)}) collective-permute-start(bf16[320,128]{1,0:T(8,128)(2,1)S(1)} %get-tuple-element.47), channel_id=1, source_target_pairs={{0,4},{1,5},{4,8},{5,9},{8,12},{9,13},{12,0},{13,1},{2,6},{3,7},{6... | collective-permute-start | bytes 245768 | tf_op jit(solution)/shard_map/ppermute | solution.py:675
  55.8 5.9 %collective-permute-done.9.refs_2_ = bf16[320,128]{1,0:T(8,128)(2,1)S(1)} collective-permute-done((bf16[320,128]{1,0:T(8,128)(2,1)S(1)}, bf16[320,128]{1,0:T(8,128)(2,1)S(1)}, u32[]{:S(2)}, u32[]{:S(2)}) %collective-permute-start.9) | collective-permute-done | bytes 81952 | tf_op jit(solution)/shard_map/ppermute | solution.py:675
  61.7 2.1 %shard_map.143 = (bf16[144,16,128]{2,1,0:T(8,128)(2,1)}, f32[32,4,128]{2,1,0:T(4,128)}, f32[32,4,128]{2,1,0:T(4,128)}) custom-call(bf16[1024,1024]{1,0:T(8,128)(2,1)S(1)} %copy-done.2, bf16[320,128]{1,0:T(8,128)(2,1)S(1)} %get-tuple-element.45.refs_0_, bf16[320,128]{1,0:T(8,128)(2,1)S(1)} %collective-permute-done.8.refs_1_, ...), custom_call_target="tpu_custom_call" | custom-call | bytes 4000000 | tf_op jit(solution)/shard_map/pallas_call | solution.py:698
  (30 shorter events, 0.1 us)
Async XLA Ops:
  0.6 1.1 %copy-start.4 = (bf16[144,16,128]{2,1,0:T(8,128)(2,1)S(1)}, bf16[144,16,128]{2,1,0:T(8,128)(2,1)}, u32[]{:S(2)}) copy-start(bf16[144,16,128]{2,1,0:T(8,128)(2,1)} %x_hbm.1) | copy-start | bytes 1769476
  1.7 0.8 %copy-start.7 = (f32[32,4,128]{2,1,0:T(4,128)S(1)}, f32[32,4,128]{2,1,0:T(4,128)}, u32[]{:S(2)}) copy-start(f32[32,4,128]{2,1,0:T(4,128)} %air_hbm.1) | copy-start | bytes 196612
  2.5 0.8 %copy-start.8 = (f32[32,4,128]{2,1,0:T(4,128)S(1)}, f32[32,4,128]{2,1,0:T(4,128)}, u32[]{:S(2)}) copy-start(f32[32,4,128]{2,1,0:T(4,128)} %ocean_hbm.1) | copy-start | bytes 196612
  3.4 0.7 %copy-start.9 = (s32[4,128]{1,0:T(4,128)S(1)}, s32[4,128]{1,0:T(4,128)}, u32[]{:S(2)}) copy-start(s32[4,128]{1,0:T(4,128)} %sea_hbm.1) | copy-start | bytes 6148
  4.1 0.7 %copy-start.10 = (f32[144]{0:T(256)S(1)}, f32[144]{0:T(256)}, u32[]{:S(2)}) copy-start(f32[144]{0:T(256)} %param.13) | copy-start | bytes 1732
  4.7 0.7 %copy-start.11 = (f32[144]{0:T(256)S(1)}, f32[144]{0:T(256)}, u32[]{:S(2)}) copy-start(f32[144]{0:T(256)} %param.14) | copy-start | bytes 1732
  6.7 7.3 %collective-permute-start = (bf16[192,128]{1,0:T(8,128)(2,1)S(1)}, bf16[192,128]{1,0:T(8,128)(2,1)S(1)}, u32[]{:S(2)}, u32[]{:S(2)}) collective-permute-start(bf16[192,128]{1,0:T(8,128)(2,1)S(1)} %get-tuple-element.29.edge_ref), channel_id=1, source_target_pairs={{0,2},{2,0},{1,3},{3,1},{4,6},{6,4},{5,7},{7,5},{8,10},{10,8},{9,1... | collective-permute-start | bytes 147464 | tf_op jit(solution)/shard_map/ppermute | solution.py:736
  9.7 1.6 %copy-start.1 = (bf16[1024,1024]{1,0:T(8,128)(2,1)S(1)}, bf16[1024,1024]{1,0:T(8,128)(2,1)}, u32[]{:S(2)}) copy-start(bf16[1024,1024]{1,0:T(8,128)(2,1)} %constant.6.clone.swap_ref) | copy-start | bytes 6291460
  11.2 13.2 %copy-start.12 = (f32[1152]{0:T(1024)S(1)}, f32[1152]{0:T(1024)}, u32[]{:S(2)}) copy-start(f32[1152]{0:T(1024)} %param.15) | copy-start | bytes 13828
  11.2 19.3 %copy-start = (bf16[1152,1152]{1,0:T(8,128)(2,1)S(1)}, bf16[1152,1152]{1,0:T(8,128)(2,1)}, u32[]{:S(2)}) copy-start(bf16[1152,1152]{1,0:T(8,128)(2,1)} %quartet_ref.1) | copy-start | bytes 7962628
  11.3 19.3 %copy-start.3 = (bf16[384,1024]{1,0:T(8,128)(2,1)S(1)}, bf16[384,1024]{1,0:T(8,128)(2,1)}, u32[]{:S(2)}) copy-start(bf16[384,1024]{1,0:T(8,128)(2,1)} %constant.7.clone.beside_ref) | copy-start | bytes 2359300
  11.3 19.4 %copy-start.5 = (bf16[512,384]{1,0:T(8,128)(2,1)S(1)}, bf16[512,384]{1,0:T(8,128)(2,1)}, u32[]{:S(2)}) copy-start(bf16[512,384]{1,0:T(8,128)(2,1)} %constant.8.clone.lateral_ref) | copy-start | bytes 1179652
  11.3 19.4 %copy-start.6 = (bf16[128,1152]{1,0:T(8,128)(2,1)S(1)}, bf16[128,1152]{1,0:T(8,128)(2,1)}, u32[]{:S(2)}) copy-start(bf16[128,1152]{1,0:T(8,128)(2,1)} %coupler_ref.1) | copy-start | bytes 884740
  14.6 47.1 %copy-start.2 = (bf16[1024,1024]{1,0:T(8,128)(2,1)S(1)}, bf16[1024,1024]{1,0:T(8,128)(2,1)}, u32[]{:S(2)}) copy-start(bf16[1024,1024]{1,0:T(8,128)(2,1)} %constant.6.clone.swap_ref) | copy-start | bytes 6291460
  14.6 6.7 %collective-permute-start.1 = (bf16[400,128]{1,0:T(8,128)(2,1)S(1)}, bf16[400,128]{1,0:T(8,128)(2,1)S(1)}, u32[]{:S(2)}, u32[]{:S(2)}) collective-permute-start(bf16[400,128]{1,0:T(8,128)(2,1)S(1)} %get-tuple-element.38), channel_id=1, source_target_pairs={{0,1},{1,4},{4,5},{5,8},{8,9},{9,12},{12,13},{13,0},{2,3},{3,6},{6... | collective-permute-start | bytes 307208 | tf_op jit(solution)/shard_map/ppermute | solution.py:675
  14.7 8.2 %collective-permute-start.2 = (bf16[400,128]{1,0:T(8,128)(2,1)S(1)}, bf16[400,128]{1,0:T(8,128)(2,1)S(1)}, u32[]{:S(2)}, u32[]{:S(2)}) collective-permute-start(bf16[400,128]{1,0:T(8,128)(2,1)S(1)} %get-tuple-element.39), channel_id=1, source_target_pairs={{0,4},{1,5},{4,8},{5,9},{8,12},{9,13},{12,0},{13,1},{2,6},{3,7},{6... | collective-permute-start | bytes 307208 | tf_op jit(solution)/shard_map/ppermute | solution.py:675
  16.3 14.1 %collective-permute-start.3 = (bf16[400,128]{1,0:T(8,128)(2,1)S(1)}, bf16[400,128]{1,0:T(8,128)(2,1)S(1)}, u32[]{:S(2)}, u32[]{:S(2)}) collective-permute-start(bf16[400,128]{1,0:T(8,128)(2,1)S(1)} %get-tuple-element.40), channel_id=1, source_target_pairs={{0,5},{1,8},{4,9},{5,12},{8,13},{9,0},{12,1},{13,4},{2,7},{3,10},{... | collective-permute-start | bytes 307208 | tf_op jit(solution)/shard_map/ppermute | solution.py:675
  18.8 11.7 %collective-permute-start.4 = (bf16[400,128]{1,0:T(8,128)(2,1)S(1)}, bf16[400,128]{1,0:T(8,128)(2,1)S(1)}, u32[]{:S(2)}, u32[]{:S(2)}) collective-permute-start(bf16[400,128]{1,0:T(8,128)(2,1)S(1)} %get-tuple-element.41), channel_id=1, source_target_pairs={{0,8},{1,9},{4,12},{5,13},{8,0},{9,1},{12,4},{13,5},{2,10},{3,11},... | collective-permute-start | bytes 307208 | tf_op jit(solution)/shard_map/ppermute | solution.py:675
  20.1 10.5 %collective-permute-start.5 = (bf16[400,128]{1,0:T(8,128)(2,1)S(1)}, bf16[400,128]{1,0:T(8,128)(2,1)S(1)}, u32[]{:S(2)}, u32[]{:S(2)}) collective-permute-start(bf16[400,128]{1,0:T(8,128)(2,1)S(1)} %get-tuple-element.42), channel_id=1, source_target_pairs={{0,9},{1,12},{4,13},{5,0},{8,1},{9,4},{12,5},{13,8},{2,11},{3,14},... | collective-permute-start | bytes 307208 | tf_op jit(solution)/shard_map/ppermute | solution.py:675
  21.3 9.3 %collective-permute-start.6 = (bf16[400,128]{1,0:T(8,128)(2,1)S(1)}, bf16[400,128]{1,0:T(8,128)(2,1)S(1)}, u32[]{:S(2)}, u32[]{:S(2)}) collective-permute-start(bf16[400,128]{1,0:T(8,128)(2,1)S(1)} %get-tuple-element.43), channel_id=1, source_target_pairs={{0,12},{1,13},{4,0},{5,1},{8,4},{9,5},{12,8},{13,9},{2,14},{3,15},... | collective-permute-start | bytes 307208 | tf_op jit(solution)/shard_map/ppermute | solution.py:675
  22.9 7.7 %collective-permute-start.7 = (bf16[400,128]{1,0:T(8,128)(2,1)S(1)}, bf16[400,128]{1,0:T(8,128)(2,1)S(1)}, u32[]{:S(2)}, u32[]{:S(2)}) collective-permute-start(bf16[400,128]{1,0:T(8,128)(2,1)S(1)} %get-tuple-element.44), channel_id=1, source_target_pairs={{0,13},{1,0},{4,1},{5,4},{8,5},{9,8},{12,9},{13,12},{2,15},{3,2},{... | collective-permute-start | bytes 307208 | tf_op jit(solution)/shard_map/ppermute | solution.py:675
  38.4 10.6 %collective-permute-start.10 = (bf16[320,128]{1,0:T(8,128)(2,1)S(1)}, bf16[320,128]{1,0:T(8,128)(2,1)S(1)}, u32[]{:S(2)}, u32[]{:S(2)}) collective-permute-start(bf16[320,128]{1,0:T(8,128)(2,1)S(1)} %get-tuple-element.48), channel_id=1, source_target_pairs={{0,5},{1,8},{4,9},{5,12},{8,13},{9,0},{12,1},{13,4},{2,7},{3,10},{... | collective-permute-start | bytes 245768 | tf_op jit(solution)/shard_map/ppermute | solution.py:675
  44.9 8.0 %collective-permute-start.11 = (bf16[320,128]{1,0:T(8,128)(2,1)S(1)}, bf16[320,128]{1,0:T(8,128)(2,1)S(1)}, u32[]{:S(2)}, u32[]{:S(2)}) collective-permute-start(bf16[320,128]{1,0:T(8,128)(2,1)S(1)} %get-tuple-element.49), channel_id=1, source_target_pairs={{0,8},{1,9},{4,12},{5,13},{8,0},{9,1},{12,4},{13,5},{2,10},{3,11},... | collective-permute-start | bytes 245768 | tf_op jit(solution)/shard_map/ppermute | solution.py:675
  46.6 9.2 %collective-permute-start.12 = (bf16[320,128]{1,0:T(8,128)(2,1)S(1)}, bf16[320,128]{1,0:T(8,128)(2,1)S(1)}, u32[]{:S(2)}, u32[]{:S(2)}) collective-permute-start(bf16[320,128]{1,0:T(8,128)(2,1)S(1)} %get-tuple-element.50), channel_id=1, source_target_pairs={{0,9},{1,12},{4,13},{5,0},{8,1},{9,4},{12,5},{13,8},{2,11},{3,14},... | collective-permute-start | bytes 245768 | tf_op jit(solution)/shard_map/ppermute | solution.py:675
  46.8 9.0 %collective-permute-start.13 = (bf16[320,128]{1,0:T(8,128)(2,1)S(1)}, bf16[320,128]{1,0:T(8,128)(2,1)S(1)}, u32[]{:S(2)}, u32[]{:S(2)}) collective-permute-start(bf16[320,128]{1,0:T(8,128)(2,1)S(1)} %get-tuple-element.51), channel_id=1, source_target_pairs={{0,12},{1,13},{4,0},{5,1},{8,4},{9,5},{12,8},{13,9},{2,14},{3,15},... | collective-permute-start | bytes 245768 | tf_op jit(solution)/shard_map/ppermute | solution.py:675
  48.7 7.1 %collective-permute-start.14 = (bf16[320,128]{1,0:T(8,128)(2,1)S(1)}, bf16[320,128]{1,0:T(8,128)(2,1)S(1)}, u32[]{:S(2)}, u32[]{:S(2)}) collective-permute-start(bf16[320,128]{1,0:T(8,128)(2,1)S(1)} %get-tuple-element.52), channel_id=1, source_target_pairs={{0,13},{1,0},{4,1},{5,4},{8,5},{9,8},{12,9},{13,12},{2,15},{3,2},{... | collective-permute-start | bytes 245768 | tf_op jit(solution)/shard_map/ppermute | solution.py:675
  49.0 6.8 %collective-permute-start.8 = (bf16[320,128]{1,0:T(8,128)(2,1)S(1)}, bf16[320,128]{1,0:T(8,128)(2,1)S(1)}, u32[]{:S(2)}, u32[]{:S(2)}) collective-permute-start(bf16[320,128]{1,0:T(8,128)(2,1)S(1)} %get-tuple-element.46), channel_id=1, source_target_pairs={{0,1},{1,4},{4,5},{5,8},{8,9},{9,12},{12,13},{13,0},{2,3},{3,6},{6... | collective-permute-start | bytes 245768 | tf_op jit(solution)/shard_map/ppermute | solution.py:675
  52.9 8.8 %collective-permute-start.9 = (bf16[320,128]{1,0:T(8,128)(2,1)S(1)}, bf16[320,128]{1,0:T(8,128)(2,1)S(1)}, u32[]{:S(2)}, u32[]{:S(2)}) collective-permute-start(bf16[320,128]{1,0:T(8,128)(2,1)S(1)} %get-tuple-element.47), channel_id=1, source_target_pairs={{0,4},{1,5},{4,8},{5,9},{8,12},{9,13},{12,0},{13,1},{2,6},{3,7},{6... | collective-permute-start | bytes 245768 | tf_op jit(solution)/shard_map/ppermute | solution.py:675
where the time goes:
time: 64.2 us; the launch traced here: 63.9 us
  starting transfers between devices  26.6 us (41%)
  waiting for transfers between devices  15.6 us (24%)
  Pallas kernels  14.4 us (22%)
  local copies, waits for them, and re-layouts  6.4 us (10%)
  between operations  0.77 us (1%)
    ppermute x14, starting transfers between devices, spread_out(): received.append(lax.ppermute(pieces[shift], axes, pairs))  23.6 us
    ppermute x14, waiting for transfers between devices, spread_out(): received.append(lax.ppermute(pieces[shift], axes, pairs))  15.6 us
    pallas_call x5, Pallas kernels, call(): pl.pallas_call(kernel, out_shape=outs, in_specs=specs or [whole] * len(ar...  14.4 us
    unnamed x26, local copies, waits for them, and re-layouts  6.39 us
    ppermute x1, starting transfers between devices, by_columns(): halo = lax.ppermute(edge, 'sect', [(0, 1), (1, 0)])  3 us
  transfers between devices with their start and end apart: 15, of which 4 were waited for; matrix products, arithmetic and copies ran while one was open for 0% of the time, Pallas kernels for 4%

commit v1 on v0

--- a/solution.py
+++ b/solution.py
@@ -182,28 +182,32 @@
     return matrix
 
 
+def started(pairs, sems):
+    copies = [pltpu.make_async_copy(*pair, sems.at[i]) for i, pair in enumerate(pairs)]
+    for copy in copies:
+        copy.start()
+    return copies
+
+
 def edges_kernel(
-    x_hbm, air_hbm, ocean_hbm, sea_hbm, courant_x_hbm, courant_y_hbm,
-    by_row_ref, edge_ref, below_ref, state_ref, courant_x_ref, courant_y_ref,
-    x_ref, air_ref, ocean_ref, sea_ref, wide, sems,
+    x_hbm, air_hbm, ocean_hbm, sea_hbm, courant_x_hbm, courant_y_hbm, all_hbm, edge_hbm,
+    x_ref, air_ref, ocean_ref, sea_ref, courant_x_ref, courant_y_ref, all_ref, wide, sems,
 ):
     comps, rows, columns = x_ref.shape
     levels, tile_rows, _ = air_ref.shape
-    copies = [
-        pltpu.make_async_copy(source, target, sems.at[index])
-        for index, (source, target) in enumerate(
-            (
-                (x_hbm, x_ref),
-                (air_hbm, air_ref),
-                (ocean_hbm, ocean_ref),
-                (sea_hbm, sea_ref),
-                (courant_x_hbm, courant_x_ref),
-                (courant_y_hbm, courant_y_ref),
-            )
-        )
-    ]
-    for copy in copies:
-        copy.start()
+    copies = started(
+        [
+            (x_hbm, x_ref),
+            (air_hbm, air_ref),
+            (ocean_hbm, ocean_ref),
+            (sea_hbm, sea_ref),
+            (courant_x_hbm, courant_x_ref),
+            (courant_y_hbm, courant_y_ref),
+        ],
+        sems.at[pl.ds(0, 6)],
+    )
+    edges = comps + 16 + levels
+    start = edges
     column, lane = iota((columns, LANES), 0), iota((columns, LANES), 1)
 
     block = within(over(lane, rows), 4)
@@ -214,18 +218,33 @@
     wide[...] = x_ref[...].astype(F32).reshape(comps * rows, columns)
     for row in range(rows):
         values = wide[pl.ds(row, comps, stride=rows), :].astype(BF16)
-        by_row_ref[row] = values
+        all_ref[start : start + comps] = values
+        start += comps
         total += moved(values, (wanted & (row_of_lane == row)).astype(BF16))
-    edge_ref[:comps] = total.astype(BF16)
+    all_ref[:comps] = total.astype(BF16)
+    leaving = started(
+        [(all_ref.at[edges:start], all_hbm.at[edges:start])], sems.at[pl.ds(6, 1)]
+    )
     for copy in copies[1:]:
         copy.wait()
     owner = jnp.where(lax.axis_index("lev") == 0, 1.0, 0.0)
     head, tail = split((air_ref[0] - ocean_ref[0]) * owner)
     sea = sea_ref[...].astype(F32) * owner
     none = jnp.zeros_like(sea)
-    edge_ref[comps : comps + 16] = jnp.concatenate([head, tail, sea, none], axis=0).astype(BF16)
+    all_ref[comps : comps + 16] = jnp.concatenate([head, tail, sea, none], axis=0).astype(BF16)
     head, tail = split((air_ref[1] - ocean_ref[1]) * owner)
-    below_ref[...] = jnp.concatenate([head, tail, none, none], axis=0).astype(BF16)
+    later = start
+    below = jnp.concatenate([head, tail, none, none], axis=0)
+    all_ref[start : start + 16] = below.astype(BF16)
+    start += 16
+    terms = []
+    for ref in (courant_x_ref, courant_y_ref):
+        for term in split(ref[...]):
+            rest = jnp.zeros((1, 2 * columns - comps), F32)
+            terms += [term[:, :columns], jnp.concatenate([term[:, columns:], rest], axis=1)]
+    terms.append(jnp.zeros((8, columns), F32))
+    all_ref[start : start + 16] = jnp.concatenate(terms, axis=0).astype(BF16)
+    start += 16
 
     values = [ref[:, row, :] for ref in (air_ref, ocean_ref) for row in range(tile_rows)]
     unit = columns // len(values)
@@ -234,9 +253,20 @@
     total = jnp.zeros((levels, LANES), F32)
     for index, value in enumerate(values):
         value = value.astype(BF16)
-        state_ref[:, index * columns : (index + 1) * columns] = value
+        all_ref[start : start + levels] = value
+        start += levels
         total += moved(value, (wanted & (over(lane, unit) == index)).astype(BF16))
-    edge_ref[comps + 16 :] = total.astype(BF16)
+    all_ref[comps + 16 : edges] = total.astype(BF16)
+    leaving += started(
+        [
+            (all_ref.at[:edges], edge_hbm),
+            (all_ref.at[:edges], all_hbm.at[:edges]),
+            (all_ref.at[later:], all_hbm.at[later:]),
+        ],
+        sems.at[pl.ds(7, 3)],
+    )
+    for copy in leaving:
+        copy.wait()
 
 
 def surface_rows(values, row_of_lane, tile_rows):
@@ -251,36 +281,54 @@
 
 
 def advect_kernel(
-    groups, count, by_row_ref, edge_ref, below_ref, state_ref, courant_x_ref, courant_y_ref, swap_ref,
-    packed_ref, cx_ref, cy_ref, gathered,
+    groups, count, rows, levels, all_ref, packed_ref, cx_ref, cy_ref, edge_ref, gathered
 ):
-    rows, comps, columns = by_row_ref.shape
-    levels = state_ref.shape[0]
+    comps = cx_ref.shape[0]
+    columns = LANES
     width = columns // count
     cells = rows * width
-    cx_ref[...] = column_of(courant_x_ref[...], LANES)
-    cy_ref[...] = column_of(courant_y_ref[...], LANES)
+    first = comps + 16 + levels
+    edge_ref[...] = all_ref[:comps]
+
+    def by_row(row):
+        row = (row + rows) % rows
+        return all_ref[first + row * comps : first + (row + 1) * comps]
+
+    below = first + rows * comps
+    terms = all_ref[below + 16 : below + 32].astype(F32)
+    for index, ref in enumerate((cx_ref, cy_ref)):
+        own = terms[4 * index : 4 * index + 4]
+        own = own[:2] + own[2:]
+        ref[...] = column_of(jnp.concatenate([own[:1], own[1:, : comps - columns]], axis=1), LANES)
     source, target = iota((columns, 2 * columns), 0), iota((columns, 2 * columns), 1)
     step = jnp.where(target < columns, -1, 1)
     sides = (source == within(target + step, columns)).astype(BF16)
     for row in range(rows):
-        here = by_row_ref[row].astype(F32)
-        beside = moved(by_row_ref[row], sides)
+        here = by_row(row).astype(F32)
+        beside = moved(by_row(row), sides)
         along = upwind(here, cx_ref[...], beside[:, :columns], beside[:, columns:])
         across = upwind(
             here,
             cy_ref[...],
-            by_row_ref[row - 1 if row else rows - 1].astype(F32),
-            by_row_ref[row + 1 if row < rows - 1 else 0].astype(F32),
+            by_row(row - 1).astype(F32),
+            by_row(row + 1).astype(F32),
         )
         tile, place = divmod(row, count)
         gathered[tile * comps : (tile + 1) * comps, place * columns : (place + 1) * columns] = (
             here - along - across
         ).astype(BF16)
-    gathered[2 * comps :, :] = state_ref[...]
+    for index in range(count):
+        start = below + 32 + index * levels
+        gathered[2 * comps :, index * columns : (index + 1) * columns] = all_ref[
+            start : start + levels
+        ]
+    source = iota((count * columns, 2 * LANES), 0)
+    lane = iota((count * columns, 2 * LANES), 1)
     for target in range(count // 2):
-        lanes = slice(2 * target * LANES, 2 * (target + 1) * LANES)
-        values = moved(gathered[...], swap_ref[:, lanes]).astype(BF16)
+        origin = over(within(lane, LANES), width) * columns + within(lane, width)
+        origin = origin + (2 * target + over(lane, LANES)) * width
+        swap = (source == origin).astype(BF16)
+        values = moved(gathered[...], swap).astype(BF16)
         for side in range(2):
             half = values[:, side * LANES : (side + 1) * LANES]
             packed_ref[2 * target + side, : 2 * comps, :] = half[: 2 * comps]
@@ -295,7 +343,7 @@
         for index, term in enumerate(split(cx_ref[span]) + split(cy_ref[span])):
             riders = jnp.where(own == 5 * rows + 4 * group + index, term, riders)
 
-    values = jnp.concatenate([edge_ref[comps : comps + 16], below_ref[...]], axis=0)
+    values = jnp.concatenate([all_ref[comps : comps + 16], all_ref[below : below + 16]], axis=0)
     spot, lanes = iota((columns, count * cells), 0), iota((columns, count * cells), 1)
     repeat = spot == over(lanes, cells) * width + within(lanes, width)
     inland = moved(values, repeat.astype(BF16))
@@ -364,7 +412,7 @@
     width = cells // rows
     half = levels // 2
     block = over(iota((comps, LANES), 1), rows)
-    near = jnp.where((block < 2) | (block >= 6), halo_ref[:comps], edge_ref[:comps])
+    near = jnp.where((block < 2) | (block >= 6), halo_ref[:comps], edge_ref[...])
     source, target = iota((LANES, 4 * LANES), 0), iota((LANES, 4 * LANES), 1)
     lane = within(target, LANES)
     row = within(lane, rows)
@@ -694,59 +742,38 @@
     def shape(*dims, kind=BF16):
         return jax.ShapeDtypeStruct(dims, kind)
 
-    def call(kernel, outs, *args, kept=(), specs=None, flops=0, mega=16):
+    def call(kernel, outs, *args, kept=(), place=whole, flops=0, mega=16):
         return pl.pallas_call(
             kernel,
             out_shape=outs,
-            in_specs=specs or [whole] * len(args),
-            out_specs=jax.tree.map(lambda _: whole, outs),
+            in_specs=[place] * len(args),
+            out_specs=jax.tree.map(lambda _: place, outs),
             scratch_shapes=list(kept),
             compiler_params=pltpu.CompilerParams(vmem_limit_bytes=mega * 1024 * 1024),
             cost_estimate=pl.CostEstimate(flops=flops, bytes_accessed=4000000, transcendentals=0),
         )(*args)
 
     swap = jnp.asarray(swap_matrix(count, width), BF16)
-    row = shape(1, comps, kind=F32)
-    by_row, edge, below, state, row_x, row_y = call(
+    edges = comps + 16 + levels_own
+    fields = (spectrum, atmosphere, ocean_state, sea_mask, courant_x[None], courant_y[None])
+    fetched = shape(edges + rows * comps + 32 + count * levels_own, LANES)
+    fetched, edge = call(
         edges_kernel,
-        (
-            shape(rows, comps, columns),
-            shape(comps + 16 + levels_own, LANES),
-            shape(16, LANES),
-            shape(levels_own, count * columns),
-            row,
-            row,
-        ),
-        spectrum,
-        atmosphere,
-        ocean_state,
-        sea_mask,
-        courant_x[None],
-        courant_y[None],
-        specs=[far] * 6,
-        kept=[
-            VMEM(spectrum.shape, BF16),
-            VMEM(atmosphere.shape, F32),
-            VMEM(ocean_state.shape, F32),
-            VMEM(sea_mask.shape, sea_mask.dtype),
-            VMEM((comps * rows, columns), F32),
-            pltpu.SemaphoreType.DMA((6,)),
-        ],
+        (fetched, shape(edges, LANES)),
+        *fields,
+        kept=[VMEM(array.shape, array.dtype) for array in fields + (fetched,)]
+        + [VMEM((comps * rows, columns), F32), pltpu.SemaphoreType.DMA((10,))],
+        place=far,
+        mega=63,
     )
     halo = lax.ppermute(edge, "sect", [(0, 1), (1, 0)])
 
     size = 2 * comps + comps // groups + 16 + levels_own + levels_own // 2
     factor = shape(comps, LANES, kind=F32)
-    packed, factor_x, factor_y = call(
-        functools.partial(advect_kernel, groups, count),
-        (shape(count, size, LANES), factor, factor),
-        by_row,
-        edge,
-        below,
-        state,
-        row_x,
-        row_y,
-        swap,
+    packed, factor_x, factor_y, edge = call(
+        functools.partial(advect_kernel, groups, count, rows, levels_own),
+        (shape(count, size, LANES), factor, factor, shape(comps, LANES)),
+        fetched,
         kept=[VMEM((2 * comps + levels_own, count * columns), BF16)],
         flops=2000000000,
     )

time: 64.2 us -> 60.2 us (0.938)
  local copies, waits for them, and re-layouts: 6.4 us -> 1.14 us
  Pallas kernels: 14.4 us -> 15.9 us
    unnamed x26 -> x14, local copies, waits for them, and re-layouts: 6.39 us -> 1.13 us
    pallas_call x5, Pallas kernels: 14.4 us -> 15.9 us  [call(): pl.pallas_call(kernel, out_shape=outs, in_specs=[place] * len(args), out_...]
where the time goes in v1:
time: 60.2 us; the launch traced here: 60 us
  starting transfers between devices  26.6 us (44%)
  Pallas kernels  15.9 us (26%)
  waiting for transfers between devices  15.6 us (26%)
  local copies, waits for them, and re-layouts  1.14 us (2%)
  between operations  0.76 us (1%)
    ppermute x14, starting transfers between devices, spread_out(): received.append(lax.ppermute(pieces[shift], axes, pairs))  23.6 us
    pallas_call x5, Pallas kernels, call(): pl.pallas_call(kernel, out_shape=outs, in_specs=[place] * len(args), out_...  15.9 us
    ppermute x14, waiting for transfers between devices, spread_out(): received.append(lax.ppermute(pieces[shift], axes, pairs))  15.6 us
    ppermute x1, starting transfers between devices, by_columns(): halo = lax.ppermute(edge, 'sect', [(0, 1), (1, 0)])  3 us
  transfers between devices with their start and end apart: 15, of which 4 were waited for; matrix products, arithmetic and copies ran while one was open for 0% of the time, Pallas kernels for 4%

profile of v1, /device:TPU:0, one launch (start us, length us, event | category | flops | bytes accessed | tf_op | source)
XLA Modules:
  0.0 60.0 jit_solution(8037509686670741740)
XLA Ops:
  0.6 2.7 %shard_map.139 = (bf16[2784,128]{1,0:T(8,128)(2,1)}, bf16[192,128]{1,0:T(8,128)(2,1)}) custom-call(bf16[144,16,128]{2,1,0:T(8,128)(2,1)} %x_hbm.1, f32[32,4,128]{2,1,0:T(4,128)} %air_hbm.1, f32[32,4,128]{2,1,0:T(4,128)} %ocean_hbm.1, s32[4,128]{1,0:T(4,128)} %sea_hbm.1, f32[1,144]{1,0:T(1,128)} %bitcast.2, f32[1,144]{1,0:T(1,128)} %bitcast.3), custom_call_target="tpu_custom_call" | custom-call | bytes 4000000 | tf_op jit(solution)/shard_map/pallas_call | solution.py:746
  3.3 3.0 %collective-permute-start = (bf16[192,128]{1,0:T(8,128)(2,1)}, bf16[192,128]{1,0:T(8,128)(2,1)S(1)}, u32[]{:S(2)}, u32[]{:S(2)}) collective-permute-start(bf16[192,128]{1,0:T(8,128)(2,1)} %get-tuple-element.28), channel_id=1, source_target_pairs={{0,2},{2,0},{1,3},{3,1},{4,6},{6,4},{5,7},{7,5},{8,10},{10,8},{9,1... | collective-permute-start | bytes 147464 | tf_op jit(solution)/shard_map/ppermute | solution.py:769
  6.3 1.1 %copy-done.5 = bf16[2784,128]{1,0:T(8,128)(2,1)S(1)} copy-done((bf16[2784,128]{1,0:T(8,128)(2,1)S(1)}, bf16[2784,128]{1,0:T(8,128)(2,1)}, u32[]{:S(2)}) %copy-start.5) | copy-done | bytes 712728
  7.4 0.0 copy-start.4
  7.4 2.7 %shard_map.140 = (bf16[8,400,128]{2,1,0:T(8,128)(2,1)S(1)}, f32[144,128]{1,0:T(8,128)S(1)}, f32[144,128]{1,0:T(8,128)S(1)}, bf16[144,128]{1,0:T(8,128)(2,1)S(1)}) custom-call(bf16[2784,128]{1,0:T(8,128)(2,1)S(1)} %copy-done.5), custom_call_target="tpu_custom_call" | custom-call | flops 2000000000 | bytes 4000000 | tf_op jit(solution)/shard_map/pallas_call | solution.py:746
  10.1 0.0 collective-permute-done.halo_ref
  10.1 0.6 %shard_map.141 = (bf16[400,128]{1,0:T(8,128)(2,1)S(1)}, bf16[400,128]{1,0:T(8,128)(2,1)S(1)}, bf16[400,128]{1,0:T(8,128)(2,1)S(1)}, bf16[400,128]{1,0:T(8,128)(2...) custom-call(bf16[8,400,128]{2,1,0:T(8,128)(2,1)S(1)} %get-tuple-elem, ...), custom_call_target="tpu_custom_call" | custom-call | bytes 4000000 | tf_op jit(solution)/shard_map/pallas_call | solution.py:746
  10.8 0.0 copy-start.1
  10.8 0.1 collective-permute-start.1
  10.9 1.6 %collective-permute-start.2 = (bf16[400,128]{1,0:T(8,128)(2,1)S(1)}, bf16[400,128]{1,0:T(8,128)(2,1)S(1)}, u32[]{:S(2)}, u32[]{:S(2)}) collective-permute-start(bf16[400,128]{1,0:T(8,128)(2,1)S(1)} %get-tuple-element.33), channel_id=1, source_target_pairs={{0,4},{1,5},{4,8},{5,9},{8,12},{9,13},{12,0},{13,1},{2,6},{3,7},{6... | collective-permute-start | bytes 307208 | tf_op jit(solution)/shard_map/ppermute | solution.py:723
  12.5 2.5 %collective-permute-start.3 = (bf16[400,128]{1,0:T(8,128)(2,1)S(1)}, bf16[400,128]{1,0:T(8,128)(2,1)S(1)}, u32[]{:S(2)}, u32[]{:S(2)}) collective-permute-start(bf16[400,128]{1,0:T(8,128)(2,1)S(1)} %get-tuple-element.34), channel_id=1, source_target_pairs={{0,5},{1,8},{4,9},{5,12},{8,13},{9,0},{12,1},{13,4},{2,7},{3,10},{... | collective-permute-start | bytes 307208 | tf_op jit(solution)/shard_map/ppermute | solution.py:723
  15.0 1.2 %collective-permute-start.4 = (bf16[400,128]{1,0:T(8,128)(2,1)S(1)}, bf16[400,128]{1,0:T(8,128)(2,1)S(1)}, u32[]{:S(2)}, u32[]{:S(2)}) collective-permute-start(bf16[400,128]{1,0:T(8,128)(2,1)S(1)} %get-tuple-element.35), channel_id=1, source_target_pairs={{0,8},{1,9},{4,12},{5,13},{8,0},{9,1},{12,4},{13,5},{2,10},{3,11},... | collective-permute-start | bytes 307208 | tf_op jit(solution)/shard_map/ppermute | solution.py:723
  16.3 1.2 %collective-permute-start.5 = (bf16[400,128]{1,0:T(8,128)(2,1)S(1)}, bf16[400,128]{1,0:T(8,128)(2,1)S(1)}, u32[]{:S(2)}, u32[]{:S(2)}) collective-permute-start(bf16[400,128]{1,0:T(8,128)(2,1)S(1)} %get-tuple-element.36), channel_id=1, source_target_pairs={{0,9},{1,12},{4,13},{5,0},{8,1},{9,4},{12,5},{13,8},{2,11},{3,14},... | collective-permute-start | bytes 307208 | tf_op jit(solution)/shard_map/ppermute | solution.py:723
  17.5 1.6 %collective-permute-start.6 = (bf16[400,128]{1,0:T(8,128)(2,1)S(1)}, bf16[400,128]{1,0:T(8,128)(2,1)S(1)}, u32[]{:S(2)}, u32[]{:S(2)}) collective-permute-start(bf16[400,128]{1,0:T(8,128)(2,1)S(1)} %get-tuple-element.37), channel_id=1, source_target_pairs={{0,12},{1,13},{4,0},{5,1},{8,4},{9,5},{12,8},{13,9},{2,14},{3,15},... | collective-permute-start | bytes 307208 | tf_op jit(solution)/shard_map/ppermute | solution.py:723
  19.1 0.0 collective-permute-done.2.refs_2_
  19.1 1.6 %collective-permute-start.7 = (bf16[400,128]{1,0:T(8,128)(2,1)S(1)}, bf16[400,128]{1,0:T(8,128)(2,1)S(1)}, u32[]{:S(2)}, u32[]{:S(2)}) collective-permute-start(bf16[400,128]{1,0:T(8,128)(2,1)S(1)} %get-tuple-element.38), channel_id=1, source_target_pairs={{0,13},{1,0},{4,1},{5,4},{8,5},{9,8},{12,9},{13,12},{2,15},{3,2},{... | collective-permute-start | bytes 307208 | tf_op jit(solution)/shard_map/ppermute | solution.py:723
  20.7 5.9 %collective-permute-done.3.refs_3_ = bf16[400,128]{1,0:T(8,128)(2,1)S(1)} collective-permute-done((bf16[400,128]{1,0:T(8,128)(2,1)S(1)}, bf16[400,128]{1,0:T(8,128)(2,1)S(1)}, u32[]{:S(2)}, u32[]{:S(2)}) %collective-permute-start.3) | collective-permute-done | bytes 102432 | tf_op jit(solution)/shard_map/ppermute | solution.py:723
  26.6 0.2 collective-permute-done.4.refs_4_
  26.8 0.0 collective-permute-done.5.refs_5_
  26.8 0.0 collective-permute-done.6.refs_6_
  26.8 0.0 collective-permute-done.7.refs_7_
  26.8 7.8 %shard_map.142 = (bf16[320,128]{1,0:T(8,128)(2,1)S(1)}, bf16[320,128]{1,0:T(8,128)(2,1)S(1)}, bf16[320,128]{1,0:T(8,128)(2,1)S(1)}, bf16[320,128]{1,0:T(8,128)(2...) custom-call(bf16[1152,1152]{1,0:T(8,128)(2,1)S(1)} %copy-done, ...), custom_call_target="tpu_custom_call" | custom-call | bytes 4000000 | tf_op jit(solution)/shard_map/pallas_call | solution.py:746
  34.6 6.4 %collective-permute-start.10 = (bf16[320,128]{1,0:T(8,128)(2,1)S(1)}, bf16[320,128]{1,0:T(8,128)(2,1)S(1)}, u32[]{:S(2)}, u32[]{:S(2)}) collective-permute-start(bf16[320,128]{1,0:T(8,128)(2,1)S(1)} %get-tuple-element.42), channel_id=1, source_target_pairs={{0,5},{1,8},{4,9},{5,12},{8,13},{9,0},{12,1},{13,4},{2,7},{3,10},{... | collective-permute-start | bytes 245768 | tf_op jit(solution)/shard_map/ppermute | solution.py:723
  41.0 1.7 %collective-permute-start.11 = (bf16[320,128]{1,0:T(8,128)(2,1)S(1)}, bf16[320,128]{1,0:T(8,128)(2,1)S(1)}, u32[]{:S(2)}, u32[]{:S(2)}) collective-permute-start(bf16[320,128]{1,0:T(8,128)(2,1)S(1)} %get-tuple-element.43), channel_id=1, source_target_pairs={{0,8},{1,9},{4,12},{5,13},{8,0},{9,1},{12,4},{13,5},{2,10},{3,11},... | collective-permute-start | bytes 245768 | tf_op jit(solution)/shard_map/ppermute | solution.py:723
  42.8 0.2 collective-permute-start.12
  43.0 1.9 %collective-permute-start.13 = (bf16[320,128]{1,0:T(8,128)(2,1)S(1)}, bf16[320,128]{1,0:T(8,128)(2,1)S(1)}, u32[]{:S(2)}, u32[]{:S(2)}) collective-permute-start(bf16[320,128]{1,0:T(8,128)(2,1)S(1)} %get-tuple-element.45), channel_id=1, source_target_pairs={{0,12},{1,13},{4,0},{5,1},{8,4},{9,5},{12,8},{13,9},{2,14},{3,15},... | collective-permute-start | bytes 245768 | tf_op jit(solution)/shard_map/ppermute | solution.py:723
  44.9 0.3 collective-permute-start.14
  45.2 0.2 collective-permute-start.8
  45.4 3.7 %collective-permute-done.11.refs_4_ = bf16[320,128]{1,0:T(8,128)(2,1)S(1)} collective-permute-done((bf16[320,128]{1,0:T(8,128)(2,1)S(1)}, bf16[320,128]{1,0:T(8,128)(2,1)S(1)}, u32[]{:S(2)}, u32[]{:S(2)}) %collective-permute-start.11) | collective-permute-done | bytes 81952 | tf_op jit(solution)/shard_map/ppermute | solution.py:723
  49.1 2.9 %collective-permute-start.9 = (bf16[320,128]{1,0:T(8,128)(2,1)S(1)}, bf16[320,128]{1,0:T(8,128)(2,1)S(1)}, u32[]{:S(2)}, u32[]{:S(2)}) collective-permute-start(bf16[320,128]{1,0:T(8,128)(2,1)S(1)} %get-tuple-element.41), channel_id=1, source_target_pairs={{0,4},{1,5},{4,8},{5,9},{8,12},{9,13},{12,0},{13,1},{2,6},{3,7},{6... | collective-permute-start | bytes 245768 | tf_op jit(solution)/shard_map/ppermute | solution.py:723
  52.0 5.9 %collective-permute-done.9.refs_2_ = bf16[320,128]{1,0:T(8,128)(2,1)S(1)} collective-permute-done((bf16[320,128]{1,0:T(8,128)(2,1)S(1)}, bf16[320,128]{1,0:T(8,128)(2,1)S(1)}, u32[]{:S(2)}, u32[]{:S(2)}) %collective-permute-start.9) | collective-permute-done | bytes 81952 | tf_op jit(solution)/shard_map/ppermute | solution.py:723
  57.9 2.1 %shard_map.143 = (bf16[144,16,128]{2,1,0:T(8,128)(2,1)}, f32[32,4,128]{2,1,0:T(4,128)}, f32[32,4,128]{2,1,0:T(4,128)}) custom-call(bf16[1024,1024]{1,0:T(8,128)(2,1)S(1)} %copy-done.1, bf16[320,128]{1,0:T(8,128)(2,1)S(1)} %get-tuple-element.39.refs_0_, bf16[320,128]{1,0:T(8,128)(2,1)S(1)} %collective-permute-done.8.refs_1_, ...), custom_call_target="tpu_custom_call" | custom-call | bytes 4000000 | tf_op jit(solution)/shard_map/pallas_call | solution.py:746
  (18 shorter events, 0.0 us)
Async XLA Ops:
  3.3 6.8 %collective-permute-start = (bf16[192,128]{1,0:T(8,128)(2,1)}, bf16[192,128]{1,0:T(8,128)(2,1)S(1)}, u32[]{:S(2)}, u32[]{:S(2)}) collective-permute-start(bf16[192,128]{1,0:T(8,128)(2,1)} %get-tuple-element.28), channel_id=1, source_target_pairs={{0,2},{2,0},{1,3},{3,1},{4,6},{6,4},{5,7},{7,5},{8,10},{10,8},{9,1... | collective-permute-start | bytes 147464 | tf_op jit(solution)/shard_map/ppermute | solution.py:769
  6.3 1.1 %copy-start.5 = (bf16[2784,128]{1,0:T(8,128)(2,1)S(1)}, bf16[2784,128]{1,0:T(8,128)(2,1)}, u32[]{:S(2)}) copy-start(bf16[2784,128]{1,0:T(8,128)(2,1)} %get-tuple-element.25.all_ref) | copy-start | bytes 2138116
  7.4 13.3 %copy-start.6 = (f32[1152]{0:T(1024)S(1)}, f32[1152]{0:T(1024)}, u32[]{:S(2)}) copy-start(f32[1152]{0:T(1024)} %param.15) | copy-start | bytes 13828
  7.4 19.4 %copy-start = (bf16[1152,1152]{1,0:T(8,128)(2,1)S(1)}, bf16[1152,1152]{1,0:T(8,128)(2,1)}, u32[]{:S(2)}) copy-start(bf16[1152,1152]{1,0:T(8,128)(2,1)} %quartet_ref.1) | copy-start | bytes 7962628
  7.4 19.4 %copy-start.2 = (bf16[384,1024]{1,0:T(8,128)(2,1)S(1)}, bf16[384,1024]{1,0:T(8,128)(2,1)}, u32[]{:S(2)}) copy-start(bf16[384,1024]{1,0:T(8,128)(2,1)} %constant.7.clone.beside_ref) | copy-start | bytes 2359300
  7.4 19.4 %copy-start.3 = (bf16[512,384]{1,0:T(8,128)(2,1)S(1)}, bf16[512,384]{1,0:T(8,128)(2,1)}, u32[]{:S(2)}) copy-start(bf16[512,384]{1,0:T(8,128)(2,1)} %constant.8.clone.lateral_ref) | copy-start | bytes 1179652
  7.4 19.4 %copy-start.4 = (bf16[128,1152]{1,0:T(8,128)(2,1)S(1)}, bf16[128,1152]{1,0:T(8,128)(2,1)}, u32[]{:S(2)}) copy-start(bf16[128,1152]{1,0:T(8,128)(2,1)} %coupler_ref.1) | copy-start | bytes 884740
  10.8 47.1 %copy-start.1 = (bf16[1024,1024]{1,0:T(8,128)(2,1)S(1)}, bf16[1024,1024]{1,0:T(8,128)(2,1)}, u32[]{:S(2)}) copy-start(bf16[1024,1024]{1,0:T(8,128)(2,1)} %constant.6.clone.swap_ref) | copy-start | bytes 6291460
  10.8 6.7 %collective-permute-start.1 = (bf16[400,128]{1,0:T(8,128)(2,1)S(1)}, bf16[400,128]{1,0:T(8,128)(2,1)S(1)}, u32[]{:S(2)}, u32[]{:S(2)}) collective-permute-start(bf16[400,128]{1,0:T(8,128)(2,1)S(1)} %get-tuple-element.32), channel_id=1, source_target_pairs={{0,1},{1,4},{4,5},{5,8},{8,9},{9,12},{12,13},{13,0},{2,3},{3,6},{6... | collective-permute-start | bytes 307208 | tf_op jit(solution)/shard_map/ppermute | solution.py:723
  10.9 8.2 %collective-permute-start.2 = (bf16[400,128]{1,0:T(8,128)(2,1)S(1)}, bf16[400,128]{1,0:T(8,128)(2,1)S(1)}, u32[]{:S(2)}, u32[]{:S(2)}) collective-permute-start(bf16[400,128]{1,0:T(8,128)(2,1)S(1)} %get-tuple-element.33), channel_id=1, source_target_pairs={{0,4},{1,5},{4,8},{5,9},{8,12},{9,13},{12,0},{13,1},{2,6},{3,7},{6... | collective-permute-start | bytes 307208 | tf_op jit(solution)/shard_map/ppermute | solution.py:723
  12.5 14.1 %collective-permute-start.3 = (bf16[400,128]{1,0:T(8,128)(2,1)S(1)}, bf16[400,128]{1,0:T(8,128)(2,1)S(1)}, u32[]{:S(2)}, u32[]{:S(2)}) collective-permute-start(bf16[400,128]{1,0:T(8,128)(2,1)S(1)} %get-tuple-element.34), channel_id=1, source_target_pairs={{0,5},{1,8},{4,9},{5,12},{8,13},{9,0},{12,1},{13,4},{2,7},{3,10},{... | collective-permute-start | bytes 307208 | tf_op jit(solution)/shard_map/ppermute | solution.py:723
  15.0 11.7 %collective-permute-start.4 = (bf16[400,128]{1,0:T(8,128)(2,1)S(1)}, bf16[400,128]{1,0:T(8,128)(2,1)S(1)}, u32[]{:S(2)}, u32[]{:S(2)}) collective-permute-start(bf16[400,128]{1,0:T(8,128)(2,1)S(1)} %get-tuple-element.35), channel_id=1, source_target_pairs={{0,8},{1,9},{4,12},{5,13},{8,0},{9,1},{12,4},{13,5},{2,10},{3,11},... | collective-permute-start | bytes 307208 | tf_op jit(solution)/shard_map/ppermute | solution.py:723
  16.3 10.5 %collective-permute-start.5 = (bf16[400,128]{1,0:T(8,128)(2,1)S(1)}, bf16[400,128]{1,0:T(8,128)(2,1)S(1)}, u32[]{:S(2)}, u32[]{:S(2)}) collective-permute-start(bf16[400,128]{1,0:T(8,128)(2,1)S(1)} %get-tuple-element.36), channel_id=1, source_target_pairs={{0,9},{1,12},{4,13},{5,0},{8,1},{9,4},{12,5},{13,8},{2,11},{3,14},... | collective-permute-start | bytes 307208 | tf_op jit(solution)/shard_map/ppermute | solution.py:723
  17.5 9.3 %collective-permute-start.6 = (bf16[400,128]{1,0:T(8,128)(2,1)S(1)}, bf16[400,128]{1,0:T(8,128)(2,1)S(1)}, u32[]{:S(2)}, u32[]{:S(2)}) collective-permute-start(bf16[400,128]{1,0:T(8,128)(2,1)S(1)} %get-tuple-element.37), channel_id=1, source_target_pairs={{0,12},{1,13},{4,0},{5,1},{8,4},{9,5},{12,8},{13,9},{2,14},{3,15},... | collective-permute-start | bytes 307208 | tf_op jit(solution)/shard_map/ppermute | solution.py:723
  19.1 7.7 %collective-permute-start.7 = (bf16[400,128]{1,0:T(8,128)(2,1)S(1)}, bf16[400,128]{1,0:T(8,128)(2,1)S(1)}, u32[]{:S(2)}, u32[]{:S(2)}) collective-permute-start(bf16[400,128]{1,0:T(8,128)(2,1)S(1)} %get-tuple-element.38), channel_id=1, source_target_pairs={{0,13},{1,0},{4,1},{5,4},{8,5},{9,8},{12,9},{13,12},{2,15},{3,2},{... | collective-permute-start | bytes 307208 | tf_op jit(solution)/shard_map/ppermute | solution.py:723
  34.6 10.6 %collective-permute-start.10 = (bf16[320,128]{1,0:T(8,128)(2,1)S(1)}, bf16[320,128]{1,0:T(8,128)(2,1)S(1)}, u32[]{:S(2)}, u32[]{:S(2)}) collective-permute-start(bf16[320,128]{1,0:T(8,128)(2,1)S(1)} %get-tuple-element.42), channel_id=1, source_target_pairs={{0,5},{1,8},{4,9},{5,12},{8,13},{9,0},{12,1},{13,4},{2,7},{3,10},{... | collective-permute-start | bytes 245768 | tf_op jit(solution)/shard_map/ppermute | solution.py:723
  41.0 8.0 %collective-permute-start.11 = (bf16[320,128]{1,0:T(8,128)(2,1)S(1)}, bf16[320,128]{1,0:T(8,128)(2,1)S(1)}, u32[]{:S(2)}, u32[]{:S(2)}) collective-permute-start(bf16[320,128]{1,0:T(8,128)(2,1)S(1)} %get-tuple-element.43), channel_id=1, source_target_pairs={{0,8},{1,9},{4,12},{5,13},{8,0},{9,1},{12,4},{13,5},{2,10},{3,11},... | collective-permute-start | bytes 245768 | tf_op jit(solution)/shard_map/ppermute | solution.py:723
  42.8 9.3 %collective-permute-start.12 = (bf16[320,128]{1,0:T(8,128)(2,1)S(1)}, bf16[320,128]{1,0:T(8,128)(2,1)S(1)}, u32[]{:S(2)}, u32[]{:S(2)}) collective-permute-start(bf16[320,128]{1,0:T(8,128)(2,1)S(1)} %get-tuple-element.44), channel_id=1, source_target_pairs={{0,9},{1,12},{4,13},{5,0},{8,1},{9,4},{12,5},{13,8},{2,11},{3,14},... | collective-permute-start | bytes 245768 | tf_op jit(solution)/shard_map/ppermute | solution.py:723
  43.0 9.1 %collective-permute-start.13 = (bf16[320,128]{1,0:T(8,128)(2,1)S(1)}, bf16[320,128]{1,0:T(8,128)(2,1)S(1)}, u32[]{:S(2)}, u32[]{:S(2)}) collective-permute-start(bf16[320,128]{1,0:T(8,128)(2,1)S(1)} %get-tuple-element.45), channel_id=1, source_target_pairs={{0,12},{1,13},{4,0},{5,1},{8,4},{9,5},{12,8},{13,9},{2,14},{3,15},... | collective-permute-start | bytes 245768 | tf_op jit(solution)/shard_map/ppermute | solution.py:723
  44.9 7.1 %collective-permute-start.14 = (bf16[320,128]{1,0:T(8,128)(2,1)S(1)}, bf16[320,128]{1,0:T(8,128)(2,1)S(1)}, u32[]{:S(2)}, u32[]{:S(2)}) collective-permute-start(bf16[320,128]{1,0:T(8,128)(2,1)S(1)} %get-tuple-element.46), channel_id=1, source_target_pairs={{0,13},{1,0},{4,1},{5,4},{8,5},{9,8},{12,9},{13,12},{2,15},{3,2},{... | collective-permute-start | bytes 245768 | tf_op jit(solution)/shard_map/ppermute | solution.py:723
  45.2 6.8 %collective-permute-start.8 = (bf16[320,128]{1,0:T(8,128)(2,1)S(1)}, bf16[320,128]{1,0:T(8,128)(2,1)S(1)}, u32[]{:S(2)}, u32[]{:S(2)}) collective-permute-start(bf16[320,128]{1,0:T(8,128)(2,1)S(1)} %get-tuple-element.40), channel_id=1, source_target_pairs={{0,1},{1,4},{4,5},{5,8},{8,9},{9,12},{12,13},{13,0},{2,3},{3,6},{6... | collective-permute-start | bytes 245768 | tf_op jit(solution)/shard_map/ppermute | solution.py:723
  49.1 8.8 %collective-permute-start.9 = (bf16[320,128]{1,0:T(8,128)(2,1)S(1)}, bf16[320,128]{1,0:T(8,128)(2,1)S(1)}, u32[]{:S(2)}, u32[]{:S(2)}) collective-permute-start(bf16[320,128]{1,0:T(8,128)(2,1)S(1)} %get-tuple-element.41), channel_id=1, source_target_pairs={{0,4},{1,5},{4,8},{5,9},{8,12},{9,13},{12,0},{13,1},{2,6},{3,7},{6... | collective-permute-start | bytes 245768 | tf_op jit(solution)/shard_map/ppermute | solution.py:723

commit v2 on v1

--- a/solution.py
+++ b/solution.py
@@ -269,17 +269,6 @@
         copy.wait()
 
 
-def surface_rows(values, row_of_lane, tile_rows):
-    first_row = lax.axis_index("cells") * tile_rows
-    kept = row_of_lane == first_row + within(iota(values.shape, 0), tile_rows)
-    kept = jnp.where(kept, values, 0.0).astype(BF16)
-    target = iota((8, values.shape[0]), 0)
-    source = over(iota((8, values.shape[0]), 1), tile_rows)
-    source = jnp.where(source < 3, source, jnp.where(source < 4, 7, source - 1))
-    adds = (target == jnp.where(source < 5, source, 7)).astype(BF16)
-    return jnp.dot(adds, kept, preferred_element_type=F32)
-
-
 def advect_kernel(
     groups, count, rows, levels, all_ref, packed_ref, cx_ref, cy_ref, edge_ref, gathered
 ):
@@ -332,7 +321,7 @@
         for side in range(2):
             half = values[:, side * LANES : (side + 1) * LANES]
             packed_ref[2 * target + side, : 2 * comps, :] = half[: 2 * comps]
-            start = 2 * comps + comps // groups + 16
+            start = 2 * comps + comps // groups
             packed_ref[2 * target + side, start : start + levels, :] = half[2 * comps :]
     size = comps // groups
 
@@ -344,19 +333,19 @@
             riders = jnp.where(own == 5 * rows + 4 * group + index, term, riders)
 
     values = jnp.concatenate([all_ref[comps : comps + 16], all_ref[below : below + 16]], axis=0)
-    spot, lanes = iota((columns, count * cells), 0), iota((columns, count * cells), 1)
-    repeat = spot == over(lanes, cells) * width + within(lanes, width)
-    inland = moved(values, repeat.astype(BF16))
-    inland = surface_rows(inland, over(within(iota(inland.shape, 1), cells), width), 4)
     spot, lanes = iota((columns, count * LANES), 0), iota((columns, count * LANES), 1)
-    first = over(lanes, LANES) * width
-    lanes = within(lanes, LANES)
-    repeat = ((lanes < rows) & (spot == first - 1)) | (
-        (lanes >= LANES - rows) & (spot == first + width)
-    )
-    shore = moved(values, repeat.astype(BF16))
-    shore = surface_rows(shore, within(iota(shore.shape, 1), rows), 4)
-    place = iota((8, LANES), 0)
+    first_column = over(lanes, LANES) * width
+    lanes = within(lanes, LANES) - 6 * rows
+    inside = (lanes >= 0) & (lanes < width) & (spot == first_column + lanes)
+    inland = moved(values, inside.astype(BF16))
+    outside = ((lanes == 0) & (spot == first_column - 1)) | (
+        (lanes == 1) & (spot == first_column + width)
+    )
+    shore = moved(values[:16], outside.astype(BF16))
+    surfaces = [inland, shore]
+    if size > 48:
+        surfaces.append(jnp.zeros((size - 48, count * LANES), F32))
+    surfaces = jnp.concatenate(surfaces, axis=0)
 
     source, target_lane = iota((cells, 2 * LANES), 0), iota((cells, 2 * LANES), 1)
     block = over(within(target_lane, LANES), rows)
@@ -386,20 +375,16 @@
                 rows_of = slice(tile * LANES, (tile + 1) * LANES)
                 total += moved(packed_ref[target, span, :], ends[group][rows_of])
         beside.append(total)
-        start = 2 * comps + size + 16
+        start = 2 * comps + size
         low = moved(packed_ref[target, start : start + half, :], shifts[0])
         high = moved(packed_ref[target, start + half : start + levels, :], shifts[1])
         beside_state.append(low + high)
     for target in range(count):
         left, right = max(target - 1, 0), min(target + 1, count - 1)
         shared = riders + beside[left][:, :LANES] + beside[right][:, LANES:]
+        shared += surfaces[:, target * LANES : (target + 1) * LANES]
         packed_ref[target, 2 * comps : 2 * comps + size, :] = shared.astype(BF16)
-        winds = [inland[:, (2 * target + i) * LANES : (2 * target + i + 1) * LANES] for i in range(2)]
-        outer = pltpu.roll(shore[:, target * LANES : (target + 1) * LANES], 5, 0)
-        winds[0] = jnp.where(place < 5, winds[0], outer)
-        start = 2 * comps + size
-        packed_ref[target, start : start + 16, :] = jnp.concatenate(winds, axis=0).astype(BF16)
-        start += 16 + levels
+        start = 2 * comps + size + levels
         outer = beside_state[left][:, :LANES] + beside_state[right][:, LANES:]
         packed_ref[target, start : start + half, :] = outer.astype(BF16)
 
@@ -448,12 +433,14 @@
         )
         spread = source == from_block * rows + within(target, rows)
         shared += moved(near[group * size : (group + 1) * size], spread.astype(BF16))
-    repeat = ((target < rows) & (source == LANES - 1)) | ((target >= LANES - rows) & (source == 0))
-    coast = moved(halo_ref[comps : comps + 16], repeat.astype(BF16))
-    coast = jnp.concatenate([coast, jnp.zeros_like(coast)], axis=0)
-    coast = surface_rows(coast, within(iota(coast.shape, 1), rows), 4)
-    coast = pltpu.roll(coast, 5, 0)
-    coast = jnp.concatenate([coast, jnp.zeros_like(coast)], axis=0)
+    beyond = ((target == 6 * rows) & (source == LANES - 1)) | (
+        (target == 6 * rows + 1) & (source == 0)
+    )
+    coast = moved(halo_ref[comps : comps + 16], beyond.astype(BF16))
+    coast = [jnp.zeros((32, LANES), F32), coast]
+    if size > 48:
+        coast.append(jnp.zeros((size - 48, LANES), F32))
+    shared += jnp.concatenate(coast, axis=0)
     inner = within(target, width)
     low = (source == target) & (inner < 4)
     high = (source == target - 8) & (inner >= 8) & (inner < 12)
@@ -463,8 +450,7 @@
     for slot in range(count):
         target = lax.rem(me + slot, count)
         out_refs[slot][...] = packed_ref[target]
-        place, lane = iota((16, LANES), 0), iota((16, LANES), 1)
-        outer = (place >= 5) & (place < 8)
+        place, lane = iota((size, LANES), 0), iota((size, LANES), 1)
 
         def patch(start, stop, where, values):
             old = out_refs[slot][start:stop].astype(F32)
@@ -476,15 +462,13 @@
                 values = ends[:, tile * LANES : (tile + 1) * LANES]
                 where = column == (width - 1 if east else 0)
                 patch(tile * comps, (tile + 1) * comps, where, values)
-            own = over(iota((size, LANES), 1), rows)
-            where = own < 0
+            own = over(lane, rows)
+            where = (place >= 32) & (place < 48) & (lane == 6 * rows + (1 if east else 0))
             for group in range(groups):
                 where = where | (own == ((2 * group + 7) % 8 if east else 2 * group))
             patch(2 * comps, 2 * comps + size, where, shared)
             start = 2 * comps + size
-            side = lane >= LANES - rows if east else lane < rows
-            patch(start, start + 16, outer & side, coast)
-            start += 16 + levels
+            start += levels
             inner = within(iota((half, LANES), 1), 8)
             patch(start, start + half, (inner >= 2) == east, state)
 
@@ -511,6 +495,8 @@
     width = cells // rows
     levels = coupler_ref.shape[0] // 2
     half = shares.shape[1]
+    lev_parts = levels // half
+    tile_rows = rows * lev_parts // count
     me = lax.axis_index(("cells", "lev"))
     west_end = (me == 0) & (lax.axis_index("sect") == 0)
     east_end = (me == count - 1) & (lax.axis_index("sect") == lax.axis_size("sect") - 1)
@@ -527,7 +513,16 @@
         rider = source - (5 * rows + 4 * group)
         rider = (rider >= 0) & (rider < 4) & (over(rider, 2) == target - LANES)
         opened.append((column | rider).astype(BF16))
-    winds = jnp.zeros((16, LANES), F32)
+    source, target = iota((LANES, wide), 0), iota((LANES, wide), 1)
+    on_side = target >= cells
+    lane = within(target, width) + 6 * rows
+    side = jnp.where(target < cells + rows, 0, 1) + 6 * rows
+    repeat = (source == jnp.where(on_side, side, lane)).astype(BF16)
+    place, target = iota((48, wide), 0), iota((48, wide), 1)
+    on_side = target >= cells
+    row_of_lane = jnp.where(on_side, within(target, rows), over(target, width))
+    row_of_lane = jnp.where((place >= 32) == on_side, row_of_lane, -1) - within(place, tile_rows)
+    terms = jnp.zeros((48, wide), F32)
     for slot in range(count):
         source = lax.rem(me - slot + count, count)
         start = pl.multiple_of(source * comps, 16)
@@ -547,22 +542,24 @@
             values = values[:, :LANES]
             first_in[span, wide + cells :] = (values * values).astype(BF16)
             factors[span, :8] = values_8
-        place = 2 * comps + size
-        winds += in_refs[slot][place : place + 16].astype(F32)
-        place += 16
+        place = 2 * comps
+        spread = moved(in_refs[slot][place : place + 48], repeat)
+        here = row_of_lane == over(source, lev_parts) * tile_rows
+        terms += jnp.where(here, spread, 0.0)
+        place += size
         state[source] = in_refs[slot][place : place + half]
         ends[source] = in_refs[slot][place + half :]
 
-    first, second = winds[:8], winds[8:]
-    outer = pltpu.roll(first, 3, 0)
-
-    def joined(tile):
-        return tile[:1] + tile[1:2]
-
-    surface = jnp.concatenate([joined(first), joined(second), joined(outer)], axis=1)
-    terms = jnp.concatenate([first, second, outer], axis=1)
-    sea = terms[2:3]
-    below = jnp.concatenate([joined(first[3:5]), joined(second[3:5])], axis=1)
+    place, source = iota((8, 48), 0), over(iota((8, 48), 1), tile_rows)
+    source = jnp.where(source < 3, source, jnp.where(source < 8, source - 1, source - 8))
+    skipped = over(iota((8, 48), 1), tile_rows) == 3
+    terms = moved((place == jnp.where(skipped, 8, source)).astype(F32), terms.astype(BF16))
+
+    def joined(rows_of):
+        return rows_of[:1] + rows_of[1:2]
+
+    surface, sea = joined(terms), terms[2:3]
+    below = joined(terms[3:5])[:, :cells]
     wind = surface * surface
 
     def renew(values, products, growth, wind, sea):
@@ -595,7 +592,6 @@
         values = values.astype(F32)
         second_in[span, cells:] = (values * values).astype(BF16)
 
-    lev_parts = levels // half
     halves = iota((half, LANES), 1) < LANES // 2
 
     def collected(values):
@@ -735,7 +731,7 @@
     width = columns // count
     cells = rows * width
     levels_own, tile_rows, _ = atmosphere.shape
-    groups = 3 if comps % 48 == 0 else 2
+    groups = 3
     whole = pl.BlockSpec(memory_space=VMEM)
     far = pl.BlockSpec(memory_space=pltpu.HBM)
 
@@ -768,7 +764,7 @@
     )
     halo = lax.ppermute(edge, "sect", [(0, 1), (1, 0)])
 
-    size = 2 * comps + comps // groups + 16 + levels_own + levels_own // 2
+    size = 2 * comps + comps // groups + levels_own + levels_own // 2
     factor = shape(comps, LANES, kind=F32)
     packed, factor_x, factor_y, edge = call(
         functools.partial(advect_kernel, groups, count, rows, levels_own),
@@ -838,7 +834,8 @@
         and lax.axis_size("sect") == 2
         and rows * (columns // blocks) == 2 * LANES
         and atmosphere.shape[1] * (columns // blocks) * 2 == LANES
-        and any(comps % (16 * groups) == 0 for groups in (3, 2))
+        and comps % 48 == 0
+        and comps >= 144
         and atmosphere.shape[0] % 16 == 0
         and NSTEP == 2
     )

time: 60.2 us -> 59 us (0.980)
  no operation moved by 1% of the time
where the time goes in v2:
time: 59 us; the launch traced here: 58.8 us
  starting transfers between devices  26.1 us (44%)
  waiting for transfers between devices  15.6 us (26%)
  Pallas kernels  15.3 us (26%)
  local copies, waits for them, and re-layouts  1.14 us (2%)
  between operations  0.76 us (1%)
    ppermute x14, starting transfers between devices, spread_out(): received.append(lax.ppermute(pieces[shift], axes, pairs))  23 us
    ppermute x14, waiting for transfers between devices, spread_out(): received.append(lax.ppermute(pieces[shift], axes, pairs))  15.6 us
    pallas_call x5, Pallas kernels, call(): pl.pallas_call(kernel, out_shape=outs, in_specs=[place] * len(args), out_...  15.3 us
    ppermute x1, starting transfers between devices, by_columns(): halo = lax.ppermute(edge, 'sect', [(0, 1), (1, 0)])  3 us
  transfers between devices with their start and end apart: 15, of which 4 were waited for; matrix products, arithmetic and copies ran while one was open for 0% of the time, Pallas kernels for 4%

profile of v2, /device:TPU:0, one launch (start us, length us, event | category | flops | bytes accessed | tf_op | source)
XLA Modules:
  0.0 58.8 jit_solution(12567043453144581274)
XLA Ops:
  0.6 2.7 %shard_map.139 = (bf16[2784,128]{1,0:T(8,128)(2,1)}, bf16[192,128]{1,0:T(8,128)(2,1)}) custom-call(bf16[144,16,128]{2,1,0:T(8,128)(2,1)} %x_hbm.1, f32[32,4,128]{2,1,0:T(4,128)} %air_hbm.1, f32[32,4,128]{2,1,0:T(4,128)} %ocean_hbm.1, s32[4,128]{1,0:T(4,128)} %sea_hbm.1, f32[1,144]{1,0:T(1,128)} %bitcast.2, f32[1,144]{1,0:T(1,128)} %bitcast.3), custom_call_target="tpu_custom_call" | custom-call | bytes 4000000 | tf_op jit(solution)/shard_map/pallas_call | solution.py:742
  3.3 3.0 %collective-permute-start = (bf16[192,128]{1,0:T(8,128)(2,1)}, bf16[192,128]{1,0:T(8,128)(2,1)S(1)}, u32[]{:S(2)}, u32[]{:S(2)}) collective-permute-start(bf16[192,128]{1,0:T(8,128)(2,1)} %get-tuple-element.28), channel_id=1, source_target_pairs={{0,2},{2,0},{1,3},{3,1},{4,6},{6,4},{5,7},{7,5},{8,10},{10,8},{9,1... | collective-permute-start | bytes 147464 | tf_op jit(solution)/shard_map/ppermute | solution.py:765
  6.3 1.1 %copy-done.5 = bf16[2784,128]{1,0:T(8,128)(2,1)S(1)} copy-done((bf16[2784,128]{1,0:T(8,128)(2,1)S(1)}, bf16[2784,128]{1,0:T(8,128)(2,1)}, u32[]{:S(2)}) %copy-start.5) | copy-done | bytes 712728
  7.4 0.0 copy-start.4
  7.4 2.4 %shard_map.140 = (bf16[8,384,128]{2,1,0:T(8,128)(2,1)S(1)}, f32[144,128]{1,0:T(8,128)S(1)}, f32[144,128]{1,0:T(8,128)S(1)}, bf16[144,128]{1,0:T(8,128)(2,1)S(1)}) custom-call(bf16[2784,128]{1,0:T(8,128)(2,1)S(1)} %copy-done.5), custom_call_target="tpu_custom_call" | custom-call | flops 2000000000 | bytes 4000000 | tf_op jit(solution)/shard_map/pallas_call | solution.py:742
  9.8 0.5 shard_map.141
  10.4 0.0 copy-start.1
  10.4 0.1 collective-permute-start.1
  10.4 1.6 %collective-permute-start.2 = (bf16[384,128]{1,0:T(8,128)(2,1)S(1)}, bf16[384,128]{1,0:T(8,128)(2,1)S(1)}, u32[]{:S(2)}, u32[]{:S(2)}) collective-permute-start(bf16[384,128]{1,0:T(8,128)(2,1)S(1)} %get-tuple-element.33), channel_id=1, source_target_pairs={{0,4},{1,5},{4,8},{5,9},{8,12},{9,13},{12,0},{13,1},{2,6},{3,7},{6... | collective-permute-start | bytes 294920 | tf_op jit(solution)/shard_map/ppermute | solution.py:719
  12.1 2.5 %collective-permute-start.3 = (bf16[384,128]{1,0:T(8,128)(2,1)S(1)}, bf16[384,128]{1,0:T(8,128)(2,1)S(1)}, u32[]{:S(2)}, u32[]{:S(2)}) collective-permute-start(bf16[384,128]{1,0:T(8,128)(2,1)S(1)} %get-tuple-element.34), channel_id=1, source_target_pairs={{0,5},{1,8},{4,9},{5,12},{8,13},{9,0},{12,1},{13,4},{2,7},{3,10},{... | collective-permute-start | bytes 294920 | tf_op jit(solution)/shard_map/ppermute | solution.py:719
  14.6 1.2 %collective-permute-start.4 = (bf16[384,128]{1,0:T(8,128)(2,1)S(1)}, bf16[384,128]{1,0:T(8,128)(2,1)S(1)}, u32[]{:S(2)}, u32[]{:S(2)}) collective-permute-start(bf16[384,128]{1,0:T(8,128)(2,1)S(1)} %get-tuple-element.35), channel_id=1, source_target_pairs={{0,8},{1,9},{4,12},{5,13},{8,0},{9,1},{12,4},{13,5},{2,10},{3,11},... | collective-permute-start | bytes 294920 | tf_op jit(solution)/shard_map/ppermute | solution.py:719
  15.8 1.2 %collective-permute-start.5 = (bf16[384,128]{1,0:T(8,128)(2,1)S(1)}, bf16[384,128]{1,0:T(8,128)(2,1)S(1)}, u32[]{:S(2)}, u32[]{:S(2)}) collective-permute-start(bf16[384,128]{1,0:T(8,128)(2,1)S(1)} %get-tuple-element.36), channel_id=1, source_target_pairs={{0,9},{1,12},{4,13},{5,0},{8,1},{9,4},{12,5},{13,8},{2,11},{3,14},... | collective-permute-start | bytes 294920 | tf_op jit(solution)/shard_map/ppermute | solution.py:719
  17.0 0.0 collective-permute-done.1.refs_1_
  17.0 1.5 %collective-permute-start.6 = (bf16[384,128]{1,0:T(8,128)(2,1)S(1)}, bf16[384,128]{1,0:T(8,128)(2,1)S(1)}, u32[]{:S(2)}, u32[]{:S(2)}) collective-permute-start(bf16[384,128]{1,0:T(8,128)(2,1)S(1)} %get-tuple-element.37), channel_id=1, source_target_pairs={{0,12},{1,13},{4,0},{5,1},{8,4},{9,5},{12,8},{13,9},{2,14},{3,15},... | collective-permute-start | bytes 294920 | tf_op jit(solution)/shard_map/ppermute | solution.py:719
  18.5 1.5 %collective-permute-start.7 = (bf16[384,128]{1,0:T(8,128)(2,1)S(1)}, bf16[384,128]{1,0:T(8,128)(2,1)S(1)}, u32[]{:S(2)}, u32[]{:S(2)}) collective-permute-start(bf16[384,128]{1,0:T(8,128)(2,1)S(1)} %get-tuple-element.38), channel_id=1, source_target_pairs={{0,13},{1,0},{4,1},{5,4},{8,5},{9,8},{12,9},{13,12},{2,15},{3,2},{... | collective-permute-start | bytes 294920 | tf_op jit(solution)/shard_map/ppermute | solution.py:719
  20.1 5.7 %collective-permute-done.3.refs_3_ = bf16[384,128]{1,0:T(8,128)(2,1)S(1)} collective-permute-done((bf16[384,128]{1,0:T(8,128)(2,1)S(1)}, bf16[384,128]{1,0:T(8,128)(2,1)S(1)}, u32[]{:S(2)}, u32[]{:S(2)}) %collective-permute-start.3) | collective-permute-done | bytes 98336 | tf_op jit(solution)/shard_map/ppermute | solution.py:719
  25.7 0.2 collective-permute-done.4.refs_4_
  25.9 0.0 collective-permute-done.5.refs_5_
  25.9 0.0 collective-permute-done.6.refs_6_
  25.9 0.0 collective-permute-done.7.refs_7_
  26.0 7.6 %shard_map.142 = (bf16[320,128]{1,0:T(8,128)(2,1)S(1)}, bf16[320,128]{1,0:T(8,128)(2,1)S(1)}, bf16[320,128]{1,0:T(8,128)(2,1)S(1)}, bf16[320,128]{1,0:T(8,128)(2...) custom-call(bf16[1152,1152]{1,0:T(8,128)(2,1)S(1)} %copy-done, ...), custom_call_target="tpu_custom_call" | custom-call | bytes 4000000 | tf_op jit(solution)/shard_map/pallas_call | solution.py:742
  33.6 6.2 %collective-permute-start.10 = (bf16[320,128]{1,0:T(8,128)(2,1)S(1)}, bf16[320,128]{1,0:T(8,128)(2,1)S(1)}, u32[]{:S(2)}, u32[]{:S(2)}) collective-permute-start(bf16[320,128]{1,0:T(8,128)(2,1)S(1)} %get-tuple-element.42), channel_id=1, source_target_pairs={{0,5},{1,8},{4,9},{5,12},{8,13},{9,0},{12,1},{13,4},{2,7},{3,10},{... | collective-permute-start | bytes 245768 | tf_op jit(solution)/shard_map/ppermute | solution.py:719
  39.8 1.6 %collective-permute-start.11 = (bf16[320,128]{1,0:T(8,128)(2,1)S(1)}, bf16[320,128]{1,0:T(8,128)(2,1)S(1)}, u32[]{:S(2)}, u32[]{:S(2)}) collective-permute-start(bf16[320,128]{1,0:T(8,128)(2,1)S(1)} %get-tuple-element.43), channel_id=1, source_target_pairs={{0,8},{1,9},{4,12},{5,13},{8,0},{9,1},{12,4},{13,5},{2,10},{3,11},... | collective-permute-start | bytes 245768 | tf_op jit(solution)/shard_map/ppermute | solution.py:719
  41.5 0.3 collective-permute-start.12
  41.7 1.9 %collective-permute-start.13 = (bf16[320,128]{1,0:T(8,128)(2,1)S(1)}, bf16[320,128]{1,0:T(8,128)(2,1)S(1)}, u32[]{:S(2)}, u32[]{:S(2)}) collective-permute-start(bf16[320,128]{1,0:T(8,128)(2,1)S(1)} %get-tuple-element.45), channel_id=1, source_target_pairs={{0,12},{1,13},{4,0},{5,1},{8,4},{9,5},{12,8},{13,9},{2,14},{3,15},... | collective-permute-start | bytes 245768 | tf_op jit(solution)/shard_map/ppermute | solution.py:719
  43.6 0.3 collective-permute-start.14
  44.0 0.0 collective-permute-done.10.refs_3_
  44.0 0.2 collective-permute-start.8
  44.2 3.7 %collective-permute-done.11.refs_4_ = bf16[320,128]{1,0:T(8,128)(2,1)S(1)} collective-permute-done((bf16[320,128]{1,0:T(8,128)(2,1)S(1)}, bf16[320,128]{1,0:T(8,128)(2,1)S(1)}, u32[]{:S(2)}, u32[]{:S(2)}) %collective-permute-start.11) | collective-permute-done | bytes 81952 | tf_op jit(solution)/shard_map/ppermute | solution.py:719
  47.9 2.9 %collective-permute-start.9 = (bf16[320,128]{1,0:T(8,128)(2,1)S(1)}, bf16[320,128]{1,0:T(8,128)(2,1)S(1)}, u32[]{:S(2)}, u32[]{:S(2)}) collective-permute-start(bf16[320,128]{1,0:T(8,128)(2,1)S(1)} %get-tuple-element.41), channel_id=1, source_target_pairs={{0,4},{1,5},{4,8},{5,9},{8,12},{9,13},{12,0},{13,1},{2,6},{3,7},{6... | collective-permute-start | bytes 245768 | tf_op jit(solution)/shard_map/ppermute | solution.py:719
  50.8 6.0 %collective-permute-done.9.refs_2_ = bf16[320,128]{1,0:T(8,128)(2,1)S(1)} collective-permute-done((bf16[320,128]{1,0:T(8,128)(2,1)S(1)}, bf16[320,128]{1,0:T(8,128)(2,1)S(1)}, u32[]{:S(2)}, u32[]{:S(2)}) %collective-permute-start.9) | collective-permute-done | bytes 81952 | tf_op jit(solution)/shard_map/ppermute | solution.py:719
  56.7 2.1 %shard_map.143 = (bf16[144,16,128]{2,1,0:T(8,128)(2,1)}, f32[32,4,128]{2,1,0:T(4,128)}, f32[32,4,128]{2,1,0:T(4,128)}) custom-call(bf16[1024,1024]{1,0:T(8,128)(2,1)S(1)} %copy-done.1, bf16[320,128]{1,0:T(8,128)(2,1)S(1)} %get-tuple-element.39.refs_0_, bf16[320,128]{1,0:T(8,128)(2,1)S(1)} %collective-permute-done.8.refs_1_, ...), custom_call_target="tpu_custom_call" | custom-call | bytes 4000000 | tf_op jit(solution)/shard_map/pallas_call | solution.py:742
  (18 shorter events, 0.0 us)
Async XLA Ops:
  3.3 6.5 %collective-permute-start = (bf16[192,128]{1,0:T(8,128)(2,1)}, bf16[192,128]{1,0:T(8,128)(2,1)S(1)}, u32[]{:S(2)}, u32[]{:S(2)}) collective-permute-start(bf16[192,128]{1,0:T(8,128)(2,1)} %get-tuple-element.28), channel_id=1, source_target_pairs={{0,2},{2,0},{1,3},{3,1},{4,6},{6,4},{5,7},{7,5},{8,10},{10,8},{9,1... | collective-permute-start | bytes 147464 | tf_op jit(solution)/shard_map/ppermute | solution.py:765
  6.3 1.1 %copy-start.5 = (bf16[2784,128]{1,0:T(8,128)(2,1)S(1)}, bf16[2784,128]{1,0:T(8,128)(2,1)}, u32[]{:S(2)}) copy-start(bf16[2784,128]{1,0:T(8,128)(2,1)} %get-tuple-element.25.all_ref) | copy-start | bytes 2138116
  7.4 12.6 %copy-start.6 = (f32[1152]{0:T(1024)S(1)}, f32[1152]{0:T(1024)}, u32[]{:S(2)}) copy-start(f32[1152]{0:T(1024)} %param.15) | copy-start | bytes 13828
  7.4 18.5 %copy-start = (bf16[1152,1152]{1,0:T(8,128)(2,1)S(1)}, bf16[1152,1152]{1,0:T(8,128)(2,1)}, u32[]{:S(2)}) copy-start(bf16[1152,1152]{1,0:T(8,128)(2,1)} %quartet_ref.1) | copy-start | bytes 7962628
  7.4 18.5 %copy-start.2 = (bf16[384,1024]{1,0:T(8,128)(2,1)S(1)}, bf16[384,1024]{1,0:T(8,128)(2,1)}, u32[]{:S(2)}) copy-start(bf16[384,1024]{1,0:T(8,128)(2,1)} %constant.7.clone.beside_ref) | copy-start | bytes 2359300
  7.4 18.5 %copy-start.3 = (bf16[512,384]{1,0:T(8,128)(2,1)S(1)}, bf16[512,384]{1,0:T(8,128)(2,1)}, u32[]{:S(2)}) copy-start(bf16[512,384]{1,0:T(8,128)(2,1)} %constant.8.clone.lateral_ref) | copy-start | bytes 1179652
  7.4 18.5 %copy-start.4 = (bf16[128,1152]{1,0:T(8,128)(2,1)S(1)}, bf16[128,1152]{1,0:T(8,128)(2,1)}, u32[]{:S(2)}) copy-start(bf16[128,1152]{1,0:T(8,128)(2,1)} %coupler_ref.1) | copy-start | bytes 884740
  10.4 46.4 %copy-start.1 = (bf16[1024,1024]{1,0:T(8,128)(2,1)S(1)}, bf16[1024,1024]{1,0:T(8,128)(2,1)}, u32[]{:S(2)}) copy-start(bf16[1024,1024]{1,0:T(8,128)(2,1)} %constant.6.clone.swap_ref) | copy-start | bytes 6291460
  10.4 6.6 %collective-permute-start.1 = (bf16[384,128]{1,0:T(8,128)(2,1)S(1)}, bf16[384,128]{1,0:T(8,128)(2,1)S(1)}, u32[]{:S(2)}, u32[]{:S(2)}) collective-permute-start(bf16[384,128]{1,0:T(8,128)(2,1)S(1)} %get-tuple-element.32), channel_id=1, source_target_pairs={{0,1},{1,4},{4,5},{5,8},{8,9},{9,12},{12,13},{13,0},{2,3},{3,6},{6... | collective-permute-start | bytes 294920 | tf_op jit(solution)/shard_map/ppermute | solution.py:719
  10.4 8.1 %collective-permute-start.2 = (bf16[384,128]{1,0:T(8,128)(2,1)S(1)}, bf16[384,128]{1,0:T(8,128)(2,1)S(1)}, u32[]{:S(2)}, u32[]{:S(2)}) collective-permute-start(bf16[384,128]{1,0:T(8,128)(2,1)S(1)} %get-tuple-element.33), channel_id=1, source_target_pairs={{0,4},{1,5},{4,8},{5,9},{8,12},{9,13},{12,0},{13,1},{2,6},{3,7},{6... | collective-permute-start | bytes 294920 | tf_op jit(solution)/shard_map/ppermute | solution.py:719
  12.1 13.7 %collective-permute-start.3 = (bf16[384,128]{1,0:T(8,128)(2,1)S(1)}, bf16[384,128]{1,0:T(8,128)(2,1)S(1)}, u32[]{:S(2)}, u32[]{:S(2)}) collective-permute-start(bf16[384,128]{1,0:T(8,128)(2,1)S(1)} %get-tuple-element.34), channel_id=1, source_target_pairs={{0,5},{1,8},{4,9},{5,12},{8,13},{9,0},{12,1},{13,4},{2,7},{3,10},{... | collective-permute-start | bytes 294920 | tf_op jit(solution)/shard_map/ppermute | solution.py:719
  14.6 11.4 %collective-permute-start.4 = (bf16[384,128]{1,0:T(8,128)(2,1)S(1)}, bf16[384,128]{1,0:T(8,128)(2,1)S(1)}, u32[]{:S(2)}, u32[]{:S(2)}) collective-permute-start(bf16[384,128]{1,0:T(8,128)(2,1)S(1)} %get-tuple-element.35), channel_id=1, source_target_pairs={{0,8},{1,9},{4,12},{5,13},{8,0},{9,1},{12,4},{13,5},{2,10},{3,11},... | collective-permute-start | bytes 294920 | tf_op jit(solution)/shard_map/ppermute | solution.py:719
  15.8 10.1 %collective-permute-start.5 = (bf16[384,128]{1,0:T(8,128)(2,1)S(1)}, bf16[384,128]{1,0:T(8,128)(2,1)S(1)}, u32[]{:S(2)}, u32[]{:S(2)}) collective-permute-start(bf16[384,128]{1,0:T(8,128)(2,1)S(1)} %get-tuple-element.36), channel_id=1, source_target_pairs={{0,9},{1,12},{4,13},{5,0},{8,1},{9,4},{12,5},{13,8},{2,11},{3,14},... | collective-permute-start | bytes 294920 | tf_op jit(solution)/shard_map/ppermute | solution.py:719
  17.0 8.9 %collective-permute-start.6 = (bf16[384,128]{1,0:T(8,128)(2,1)S(1)}, bf16[384,128]{1,0:T(8,128)(2,1)S(1)}, u32[]{:S(2)}, u32[]{:S(2)}) collective-permute-start(bf16[384,128]{1,0:T(8,128)(2,1)S(1)} %get-tuple-element.37), channel_id=1, source_target_pairs={{0,12},{1,13},{4,0},{5,1},{8,4},{9,5},{12,8},{13,9},{2,14},{3,15},... | collective-permute-start | bytes 294920 | tf_op jit(solution)/shard_map/ppermute | solution.py:719
  18.5 7.4 %collective-permute-start.7 = (bf16[384,128]{1,0:T(8,128)(2,1)S(1)}, bf16[384,128]{1,0:T(8,128)(2,1)S(1)}, u32[]{:S(2)}, u32[]{:S(2)}) collective-permute-start(bf16[384,128]{1,0:T(8,128)(2,1)S(1)} %get-tuple-element.38), channel_id=1, source_target_pairs={{0,13},{1,0},{4,1},{5,4},{8,5},{9,8},{12,9},{13,12},{2,15},{3,2},{... | collective-permute-start | bytes 294920 | tf_op jit(solution)/shard_map/ppermute | solution.py:719
  33.6 10.3 %collective-permute-start.10 = (bf16[320,128]{1,0:T(8,128)(2,1)S(1)}, bf16[320,128]{1,0:T(8,128)(2,1)S(1)}, u32[]{:S(2)}, u32[]{:S(2)}) collective-permute-start(bf16[320,128]{1,0:T(8,128)(2,1)S(1)} %get-tuple-element.42), channel_id=1, source_target_pairs={{0,5},{1,8},{4,9},{5,12},{8,13},{9,0},{12,1},{13,4},{2,7},{3,10},{... | collective-permute-start | bytes 245768 | tf_op jit(solution)/shard_map/ppermute | solution.py:719
  39.8 8.0 %collective-permute-start.11 = (bf16[320,128]{1,0:T(8,128)(2,1)S(1)}, bf16[320,128]{1,0:T(8,128)(2,1)S(1)}, u32[]{:S(2)}, u32[]{:S(2)}) collective-permute-start(bf16[320,128]{1,0:T(8,128)(2,1)S(1)} %get-tuple-element.43), channel_id=1, source_target_pairs={{0,8},{1,9},{4,12},{5,13},{8,0},{9,1},{12,4},{13,5},{2,10},{3,11},... | collective-permute-start | bytes 245768 | tf_op jit(solution)/shard_map/ppermute | solution.py:719
  41.5 9.3 %collective-permute-start.12 = (bf16[320,128]{1,0:T(8,128)(2,1)S(1)}, bf16[320,128]{1,0:T(8,128)(2,1)S(1)}, u32[]{:S(2)}, u32[]{:S(2)}) collective-permute-start(bf16[320,128]{1,0:T(8,128)(2,1)S(1)} %get-tuple-element.44), channel_id=1, source_target_pairs={{0,9},{1,12},{4,13},{5,0},{8,1},{9,4},{12,5},{13,8},{2,11},{3,14},... | collective-permute-start | bytes 245768 | tf_op jit(solution)/shard_map/ppermute | solution.py:719
  41.7 9.0 %collective-permute-start.13 = (bf16[320,128]{1,0:T(8,128)(2,1)S(1)}, bf16[320,128]{1,0:T(8,128)(2,1)S(1)}, u32[]{:S(2)}, u32[]{:S(2)}) collective-permute-start(bf16[320,128]{1,0:T(8,128)(2,1)S(1)} %get-tuple-element.45), channel_id=1, source_target_pairs={{0,12},{1,13},{4,0},{5,1},{8,4},{9,5},{12,8},{13,9},{2,14},{3,15},... | collective-permute-start | bytes 245768 | tf_op jit(solution)/shard_map/ppermute | solution.py:719
  43.6 7.1 %collective-permute-start.14 = (bf16[320,128]{1,0:T(8,128)(2,1)S(1)}, bf16[320,128]{1,0:T(8,128)(2,1)S(1)}, u32[]{:S(2)}, u32[]{:S(2)}) collective-permute-start(bf16[320,128]{1,0:T(8,128)(2,1)S(1)} %get-tuple-element.46), channel_id=1, source_target_pairs={{0,13},{1,0},{4,1},{5,4},{8,5},{9,8},{12,9},{13,12},{2,15},{3,2},{... | collective-permute-start | bytes 245768 | tf_op jit(solution)/shard_map/ppermute | solution.py:719
  44.0 6.8 %collective-permute-start.8 = (bf16[320,128]{1,0:T(8,128)(2,1)S(1)}, bf16[320,128]{1,0:T(8,128)(2,1)S(1)}, u32[]{:S(2)}, u32[]{:S(2)}) collective-permute-start(bf16[320,128]{1,0:T(8,128)(2,1)S(1)} %get-tuple-element.40), channel_id=1, source_target_pairs={{0,1},{1,4},{4,5},{5,8},{8,9},{9,12},{12,13},{13,0},{2,3},{3,6},{6... | collective-permute-start | bytes 245768 | tf_op jit(solution)/shard_map/ppermute | solution.py:719
  47.9 8.9 %collective-permute-start.9 = (bf16[320,128]{1,0:T(8,128)(2,1)S(1)}, bf16[320,128]{1,0:T(8,128)(2,1)S(1)}, u32[]{:S(2)}, u32[]{:S(2)}) collective-permute-start(bf16[320,128]{1,0:T(8,128)(2,1)S(1)} %get-tuple-element.41), channel_id=1, source_target_pairs={{0,4},{1,5},{4,8},{5,9},{8,12},{9,13},{12,0},{13,1},{2,6},{3,7},{6... | collective-permute-start | bytes 245768 | tf_op jit(solution)/shard_map/ppermute | solution.py:719

commit v3 on v2

--- a/solution.py
+++ b/solution.py
@@ -448,7 +448,7 @@
     state += moved(halo_ref[comps + 16 + half :], high.astype(BF16))
     me = lax.axis_index(("cells", "lev"))
     for slot in range(count):
-        target = lax.rem(me + slot, count)
+        target = lax.rem(me + first_order(count)[slot], count)
         out_refs[slot][...] = packed_ref[target]
         place, lane = iota((size, LANES), 0), iota((size, LANES), 1)
 
@@ -524,7 +524,7 @@
     row_of_lane = jnp.where((place >= 32) == on_side, row_of_lane, -1) - within(place, tile_rows)
     terms = jnp.zeros((48, wide), F32)
     for slot in range(count):
-        source = lax.rem(me - slot + count, count)
+        source = lax.rem(me - first_order(count)[slot] + count, count)
         start = pl.multiple_of(source * comps, 16)
         span = pl.ds(start, comps)
         for tile in range(2):
@@ -676,7 +676,7 @@
             sea_part = pltpu.roll(sea_part, LANES // 2, 1)
         shares[target] = jnp.where(halves, air, sea_part).astype(BF16)
     for slot in range(count):
-        target = lax.rem(me + slot, count)
+        target = lax.rem(me + last_order(count)[slot], count)
         span = pl.ds(pl.multiple_of(target * comps, 16), comps)
         out_refs[slot][:comps] = last[span, :LANES]
         out_refs[slot][comps : 2 * comps] = last[span, LANES:]
@@ -690,7 +690,7 @@
     levels, tile_rows, _ = air_ref.shape
     me = lax.axis_index(("cells", "lev"))
     for slot in range(count):
-        source = lax.rem(me - slot + count, count)
+        source = lax.rem(me - last_order(count)[slot] + count, count)
         gathered[:, pl.ds(pl.multiple_of(source * columns, columns), columns)] = in_refs[slot][...]
     for pair in range(count // 2):
         lanes = slice(2 * pair * columns, 2 * (pair + 1) * columns)
@@ -712,11 +712,20 @@
     ocean_ref[...] = narrow[size:, :].reshape(ocean_ref.shape)
 
 
-def spread_out(pieces, axes, count):
+def first_order(count):
+    return tuple(range(count))
+
+
+def last_order(count):
+    return (0, count - 2, count - 1) + tuple(range(1, count - 2))
+
+
+def spread_out(pieces, axes, order):
+    count = len(pieces)
     received = [pieces[0]]
-    for shift in range(1, count):
-        pairs = [(index, (index + shift) % count) for index in range(count)]
-        received.append(lax.ppermute(pieces[shift], axes, pairs))
+    for slot in range(1, count):
+        pairs = [(index, (index + order[slot]) % count) for index in range(count)]
+        received.append(lax.ppermute(pieces[slot], axes, pairs))
     return received
 
 
@@ -782,7 +791,7 @@
         factor_x,
         factor_y,
     )
-    received = spread_out(pieces, axes, count)
+    received = spread_out(pieces, axes, first_order(count))
 
     results = call(
         functools.partial(steps_kernel, groups, count, rows),
@@ -805,7 +814,7 @@
         ],
         mega=32,
     )
-    returned = spread_out(results, axes, count)
+    returned = spread_out(results, axes, last_order(count))
 
     return call(
         functools.partial(finish_kernel, count),

time: 59 us -> 56.1 us (0.951)
  the two profiles are of different devices: /device:TPU:0 before, /device:TPU:9 now
where the time goes in v3:
time: 56.1 us; the launch traced here: 55.9 us
  waiting for transfers between devices  22.8 us (41%)
  starting transfers between devices  15.9 us (28%)
  Pallas kernels  15.3 us (27%)
  local copies, waits for them, and re-layouts  1.14 us (2%)
  between operations  0.72 us (1%)
    ppermute x14, waiting for transfers between devices, spread_out(): received.append(lax.ppermute(pieces[slot], axes, pairs))  22.8 us
    pallas_call x5, Pallas kernels, call(): pl.pallas_call(kernel, out_shape=outs, in_specs=[place] * len(args), out_...  15.3 us
    ppermute x14, starting transfers between devices, spread_out(): received.append(lax.ppermute(pieces[slot], axes, pairs))  14.7 us
    ppermute x1, starting transfers between devices, by_columns(): halo = lax.ppermute(edge, 'sect', [(0, 1), (1, 0)])  1.28 us
    unnamed x14, local copies, waits for them, and re-layouts  1.13 us
  transfers between devices with their start and end apart: 15, of which 8 were waited for; matrix products, arithmetic and copies ran while one was open for 0% of the time, Pallas kernels for 4%

profile of v3, /device:TPU:9, one launch (start us, length us, event | category | flops | bytes accessed | tf_op | source)
XLA Modules:
  0.0 55.9 jit_solution(10511699041005166461)
XLA Ops:
  0.6 2.7 %shard_map.139 = (bf16[2784,128]{1,0:T(8,128)(2,1)}, bf16[192,128]{1,0:T(8,128)(2,1)}) custom-call(bf16[144,16,128]{2,1,0:T(8,128)(2,1)} %x_hbm.1, f32[32,4,128]{2,1,0:T(4,128)} %air_hbm.1, f32[32,4,128]{2,1,0:T(4,128)} %ocean_hbm.1, s32[4,128]{1,0:T(4,128)} %sea_hbm.1, f32[1,144]{1,0:T(1,128)} %bitcast.2, f32[1,144]{1,0:T(1,128)} %bitcast.3), custom_call_target="tpu_custom_call" | custom-call | bytes 4000000 | tf_op jit(solution)/shard_map/pallas_call | solution.py:751
  3.3 1.3 %collective-permute-start = (bf16[192,128]{1,0:T(8,128)(2,1)}, bf16[192,128]{1,0:T(8,128)(2,1)S(1)}, u32[]{:S(2)}, u32[]{:S(2)}) collective-permute-start(bf16[192,128]{1,0:T(8,128)(2,1)} %get-tuple-element.28), channel_id=1, source_target_pairs={{0,2},{2,0},{1,3},{3,1},{4,6},{6,4},{5,7},{7,5},{8,10},{10,8},{9,1... | collective-permute-start | bytes 147464 | tf_op jit(solution)/shard_map/ppermute | solution.py:774
  4.6 1.1 %copy-done.5 = bf16[2784,128]{1,0:T(8,128)(2,1)S(1)} copy-done((bf16[2784,128]{1,0:T(8,128)(2,1)S(1)}, bf16[2784,128]{1,0:T(8,128)(2,1)}, u32[]{:S(2)}) %copy-start.5) | copy-done | bytes 712728
  5.7 0.0 copy-start.4
  5.7 2.4 %shard_map.140 = (bf16[8,384,128]{2,1,0:T(8,128)(2,1)S(1)}, f32[144,128]{1,0:T(8,128)S(1)}, f32[144,128]{1,0:T(8,128)S(1)}, bf16[144,128]{1,0:T(8,128)(2,1)S(1)}) custom-call(bf16[2784,128]{1,0:T(8,128)(2,1)S(1)} %copy-done.5), custom_call_target="tpu_custom_call" | custom-call | flops 2000000000 | bytes 4000000 | tf_op jit(solution)/shard_map/pallas_call | solution.py:751
  8.1 0.0 collective-permute-done.halo_ref
  8.1 0.5 shard_map.141
  8.6 0.0 copy-start.1
  8.6 2.2 %collective-permute-start.1 = (bf16[384,128]{1,0:T(8,128)(2,1)S(1)}, bf16[384,128]{1,0:T(8,128)(2,1)S(1)}, u32[]{:S(2)}, u32[]{:S(2)}) collective-permute-start(bf16[384,128]{1,0:T(8,128)(2,1)S(1)} %get-tuple-element.32), channel_id=1, source_target_pairs={{0,1},{1,4},{4,5},{5,8},{8,9},{9,12},{12,13},{13,0},{2,3},{3,6},{6... | collective-permute-start | bytes 294920 | tf_op jit(solution)/shard_map/ppermute | solution.py:728
  10.8 1.3 %collective-permute-start.2 = (bf16[384,128]{1,0:T(8,128)(2,1)S(1)}, bf16[384,128]{1,0:T(8,128)(2,1)S(1)}, u32[]{:S(2)}, u32[]{:S(2)}) collective-permute-start(bf16[384,128]{1,0:T(8,128)(2,1)S(1)} %get-tuple-element.33), channel_id=1, source_target_pairs={{0,4},{1,5},{4,8},{5,9},{8,12},{9,13},{12,0},{13,1},{2,6},{3,7},{6... | collective-permute-start | bytes 294920 | tf_op jit(solution)/shard_map/ppermute | solution.py:728
  12.1 0.0 collective-permute-start.3
  12.1 1.4 %collective-permute-start.4 = (bf16[384,128]{1,0:T(8,128)(2,1)S(1)}, bf16[384,128]{1,0:T(8,128)(2,1)S(1)}, u32[]{:S(2)}, u32[]{:S(2)}) collective-permute-start(bf16[384,128]{1,0:T(8,128)(2,1)S(1)} %get-tuple-element.35), channel_id=1, source_target_pairs={{0,8},{1,9},{4,12},{5,13},{8,0},{9,1},{12,4},{13,5},{2,10},{3,11},... | collective-permute-start | bytes 294920 | tf_op jit(solution)/shard_map/ppermute | solution.py:728
  13.5 1.6 %collective-permute-start.5 = (bf16[384,128]{1,0:T(8,128)(2,1)S(1)}, bf16[384,128]{1,0:T(8,128)(2,1)S(1)}, u32[]{:S(2)}, u32[]{:S(2)}) collective-permute-start(bf16[384,128]{1,0:T(8,128)(2,1)S(1)} %get-tuple-element.36), channel_id=1, source_target_pairs={{0,9},{1,12},{4,13},{5,0},{8,1},{9,4},{12,5},{13,8},{2,11},{3,14},... | collective-permute-start | bytes 294920 | tf_op jit(solution)/shard_map/ppermute | solution.py:728
  15.1 1.2 %collective-permute-start.6 = (bf16[384,128]{1,0:T(8,128)(2,1)S(1)}, bf16[384,128]{1,0:T(8,128)(2,1)S(1)}, u32[]{:S(2)}, u32[]{:S(2)}) collective-permute-start(bf16[384,128]{1,0:T(8,128)(2,1)S(1)} %get-tuple-element.37), channel_id=1, source_target_pairs={{0,12},{1,13},{4,0},{5,1},{8,4},{9,5},{12,8},{13,9},{2,14},{3,15},... | collective-permute-start | bytes 294920 | tf_op jit(solution)/shard_map/ppermute | solution.py:728
  16.3 0.4 collective-permute-start.7
  16.7 8.8 %collective-permute-done.3.refs_3_ = bf16[384,128]{1,0:T(8,128)(2,1)S(1)} collective-permute-done((bf16[384,128]{1,0:T(8,128)(2,1)S(1)}, bf16[384,128]{1,0:T(8,128)(2,1)S(1)}, u32[]{:S(2)}, u32[]{:S(2)}) %collective-permute-start.3) | collective-permute-done | bytes 98336 | tf_op jit(solution)/shard_map/ppermute | solution.py:728
  25.5 2.1 %collective-permute-done.4.refs_4_ = bf16[384,128]{1,0:T(8,128)(2,1)S(1)} collective-permute-done((bf16[384,128]{1,0:T(8,128)(2,1)S(1)}, bf16[384,128]{1,0:T(8,128)(2,1)S(1)}, u32[]{:S(2)}, u32[]{:S(2)}) %collective-permute-start.4) | collective-permute-done | bytes 98336 | tf_op jit(solution)/shard_map/ppermute | solution.py:728
  27.6 1.9 %collective-permute-done.6.refs_6_ = bf16[384,128]{1,0:T(8,128)(2,1)S(1)} collective-permute-done((bf16[384,128]{1,0:T(8,128)(2,1)S(1)}, bf16[384,128]{1,0:T(8,128)(2,1)S(1)}, u32[]{:S(2)}, u32[]{:S(2)}) %collective-permute-start.6) | collective-permute-done | bytes 98336 | tf_op jit(solution)/shard_map/ppermute | solution.py:728
  29.5 0.1 collective-permute-done.7.refs_7_
  29.7 7.6 %shard_map.142 = (bf16[320,128]{1,0:T(8,128)(2,1)S(1)}, bf16[320,128]{1,0:T(8,128)(2,1)S(1)}, bf16[320,128]{1,0:T(8,128)(2,1)S(1)}, bf16[320,128]{1,0:T(8,128)(2...) custom-call(bf16[1152,1152]{1,0:T(8,128)(2,1)S(1)} %copy-done, ...), custom_call_target="tpu_custom_call" | custom-call | bytes 4000000 | tf_op jit(solution)/shard_map/pallas_call | solution.py:751
  37.3 0.1 collective-permute-start.10
  37.4 0.7 %collective-permute-start.11 = (bf16[320,128]{1,0:T(8,128)(2,1)S(1)}, bf16[320,128]{1,0:T(8,128)(2,1)S(1)}, u32[]{:S(2)}, u32[]{:S(2)}) collective-permute-start(bf16[320,128]{1,0:T(8,128)(2,1)S(1)} %get-tuple-element.43), channel_id=1, source_target_pairs={{0,4},{1,5},{4,8},{5,9},{8,12},{9,13},{12,0},{13,1},{2,6},{3,7},{6... | collective-permute-start | bytes 245768 | tf_op jit(solution)/shard_map/ppermute | solution.py:728
  38.1 1.1 %collective-permute-start.12 = (bf16[320,128]{1,0:T(8,128)(2,1)S(1)}, bf16[320,128]{1,0:T(8,128)(2,1)S(1)}, u32[]{:S(2)}, u32[]{:S(2)}) collective-permute-start(bf16[320,128]{1,0:T(8,128)(2,1)S(1)} %get-tuple-element.44), channel_id=1, source_target_pairs={{0,5},{1,8},{4,9},{5,12},{8,13},{9,0},{12,1},{13,4},{2,7},{3,10},{... | collective-permute-start | bytes 245768 | tf_op jit(solution)/shard_map/ppermute | solution.py:728
  39.1 1.0 %collective-permute-start.13 = (bf16[320,128]{1,0:T(8,128)(2,1)S(1)}, bf16[320,128]{1,0:T(8,128)(2,1)S(1)}, u32[]{:S(2)}, u32[]{:S(2)}) collective-permute-start(bf16[320,128]{1,0:T(8,128)(2,1)S(1)} %get-tuple-element.45), channel_id=1, source_target_pairs={{0,8},{1,9},{4,12},{5,13},{8,0},{9,1},{12,4},{13,5},{2,10},{3,11},... | collective-permute-start | bytes 245768 | tf_op jit(solution)/shard_map/ppermute | solution.py:728
  40.1 1.7 %collective-permute-start.14 = (bf16[320,128]{1,0:T(8,128)(2,1)S(1)}, bf16[320,128]{1,0:T(8,128)(2,1)S(1)}, u32[]{:S(2)}, u32[]{:S(2)}) collective-permute-start(bf16[320,128]{1,0:T(8,128)(2,1)S(1)} %get-tuple-element.46), channel_id=1, source_target_pairs={{0,9},{1,12},{4,13},{5,0},{8,1},{9,4},{12,5},{13,8},{2,11},{3,14},... | collective-permute-start | bytes 245768 | tf_op jit(solution)/shard_map/ppermute | solution.py:728
  41.8 1.4 %collective-permute-start.8 = (bf16[320,128]{1,0:T(8,128)(2,1)S(1)}, bf16[320,128]{1,0:T(8,128)(2,1)S(1)}, u32[]{:S(2)}, u32[]{:S(2)}) collective-permute-start(bf16[320,128]{1,0:T(8,128)(2,1)S(1)} %get-tuple-element.40), channel_id=1, source_target_pairs={{0,12},{1,13},{4,0},{5,1},{8,4},{9,5},{12,8},{13,9},{2,14},{3,15},... | collective-permute-start | bytes 245768 | tf_op jit(solution)/shard_map/ppermute | solution.py:728
  43.2 0.7 %collective-permute-start.9 = (bf16[320,128]{1,0:T(8,128)(2,1)S(1)}, bf16[320,128]{1,0:T(8,128)(2,1)S(1)}, u32[]{:S(2)}, u32[]{:S(2)}) collective-permute-start(bf16[320,128]{1,0:T(8,128)(2,1)S(1)} %get-tuple-element.41), channel_id=1, source_target_pairs={{0,13},{1,0},{4,1},{5,4},{8,5},{9,8},{12,9},{13,12},{2,15},{3,2},{... | collective-permute-start | bytes 245768 | tf_op jit(solution)/shard_map/ppermute | solution.py:728
  43.9 5.5 %collective-permute-done.12.refs_5_ = bf16[320,128]{1,0:T(8,128)(2,1)S(1)} collective-permute-done((bf16[320,128]{1,0:T(8,128)(2,1)S(1)}, bf16[320,128]{1,0:T(8,128)(2,1)S(1)}, u32[]{:S(2)}, u32[]{:S(2)}) %collective-permute-start.12) | collective-permute-done | bytes 81952 | tf_op jit(solution)/shard_map/ppermute | solution.py:728
  49.4 1.9 %collective-permute-done.13.refs_6_ = bf16[320,128]{1,0:T(8,128)(2,1)S(1)} collective-permute-done((bf16[320,128]{1,0:T(8,128)(2,1)S(1)}, bf16[320,128]{1,0:T(8,128)(2,1)S(1)}, u32[]{:S(2)}, u32[]{:S(2)}) %collective-permute-start.13) | collective-permute-done | bytes 81952 | tf_op jit(solution)/shard_map/ppermute | solution.py:728
  51.3 2.4 %collective-permute-done.8.refs_1_ = bf16[320,128]{1,0:T(8,128)(2,1)S(1)} collective-permute-done((bf16[320,128]{1,0:T(8,128)(2,1)S(1)}, bf16[320,128]{1,0:T(8,128)(2,1)S(1)}, u32[]{:S(2)}, u32[]{:S(2)}) %collective-permute-start.8) | collective-permute-done | bytes 81952 | tf_op jit(solution)/shard_map/ppermute | solution.py:728
  53.7 0.1 collective-permute-done.9.refs_2_
  53.8 2.1 %shard_map.143 = (bf16[144,16,128]{2,1,0:T(8,128)(2,1)}, f32[32,4,128]{2,1,0:T(4,128)}, f32[32,4,128]{2,1,0:T(4,128)}) custom-call(bf16[1024,1024]{1,0:T(8,128)(2,1)S(1)} %copy-done.1, bf16[320,128]{1,0:T(8,128)(2,1)S(1)} %get-tuple-element.39.refs_0_, bf16[320,128]{1,0:T(8,128)(2,1)S(1)} %collective-permute-done.8.refs_1_, ...), custom_call_target="tpu_custom_call" | custom-call | bytes 4000000 | tf_op jit(solution)/shard_map/pallas_call | solution.py:751
  (18 shorter events, 0.0 us)
Async XLA Ops:
  3.3 4.8 %collective-permute-start = (bf16[192,128]{1,0:T(8,128)(2,1)}, bf16[192,128]{1,0:T(8,128)(2,1)S(1)}, u32[]{:S(2)}, u32[]{:S(2)}) collective-permute-start(bf16[192,128]{1,0:T(8,128)(2,1)} %get-tuple-element.28), channel_id=1, source_target_pairs={{0,2},{2,0},{1,3},{3,1},{4,6},{6,4},{5,7},{7,5},{8,10},{10,8},{9,1... | collective-permute-start | bytes 147464 | tf_op jit(solution)/shard_map/ppermute | solution.py:774
  4.6 1.1 %copy-start.5 = (bf16[2784,128]{1,0:T(8,128)(2,1)S(1)}, bf16[2784,128]{1,0:T(8,128)(2,1)}, u32[]{:S(2)}) copy-start(bf16[2784,128]{1,0:T(8,128)(2,1)} %get-tuple-element.25.all_ref) | copy-start | bytes 2138116
  5.7 11.0 %copy-start.6 = (f32[1152]{0:T(1024)S(1)}, f32[1152]{0:T(1024)}, u32[]{:S(2)}) copy-start(f32[1152]{0:T(1024)} %param.15) | copy-start | bytes 13828
  5.7 23.9 %copy-start = (bf16[1152,1152]{1,0:T(8,128)(2,1)S(1)}, bf16[1152,1152]{1,0:T(8,128)(2,1)}, u32[]{:S(2)}) copy-start(bf16[1152,1152]{1,0:T(8,128)(2,1)} %quartet_ref.1) | copy-start | bytes 7962628
  5.7 23.9 %copy-start.2 = (bf16[384,1024]{1,0:T(8,128)(2,1)S(1)}, bf16[384,1024]{1,0:T(8,128)(2,1)}, u32[]{:S(2)}) copy-start(bf16[384,1024]{1,0:T(8,128)(2,1)} %constant.7.clone.beside_ref) | copy-start | bytes 2359300
  5.7 23.9 %copy-start.3 = (bf16[512,384]{1,0:T(8,128)(2,1)S(1)}, bf16[512,384]{1,0:T(8,128)(2,1)}, u32[]{:S(2)}) copy-start(bf16[512,384]{1,0:T(8,128)(2,1)} %constant.8.clone.lateral_ref) | copy-start | bytes 1179652
  5.7 23.9 %copy-start.4 = (bf16[128,1152]{1,0:T(8,128)(2,1)S(1)}, bf16[128,1152]{1,0:T(8,128)(2,1)}, u32[]{:S(2)}) copy-start(bf16[128,1152]{1,0:T(8,128)(2,1)} %coupler_ref.1) | copy-start | bytes 884740
  8.6 45.2 %copy-start.1 = (bf16[1024,1024]{1,0:T(8,128)(2,1)S(1)}, bf16[1024,1024]{1,0:T(8,128)(2,1)}, u32[]{:S(2)}) copy-start(bf16[1024,1024]{1,0:T(8,128)(2,1)} %constant.6.clone.swap_ref) | copy-start | bytes 6291460
  8.6 6.5 %collective-permute-start.1 = (bf16[384,128]{1,0:T(8,128)(2,1)S(1)}, bf16[384,128]{1,0:T(8,128)(2,1)S(1)}, u32[]{:S(2)}, u32[]{:S(2)}) collective-permute-start(bf16[384,128]{1,0:T(8,128)(2,1)S(1)} %get-tuple-element.32), channel_id=1, source_target_pairs={{0,1},{1,4},{4,5},{5,8},{8,9},{9,12},{12,13},{13,0},{2,3},{3,6},{6... | collective-permute-start | bytes 294920 | tf_op jit(solution)/shard_map/ppermute | solution.py:728
  10.8 5.4 %collective-permute-start.2 = (bf16[384,128]{1,0:T(8,128)(2,1)S(1)}, bf16[384,128]{1,0:T(8,128)(2,1)S(1)}, u32[]{:S(2)}, u32[]{:S(2)}) collective-permute-start(bf16[384,128]{1,0:T(8,128)(2,1)S(1)} %get-tuple-element.33), channel_id=1, source_target_pairs={{0,4},{1,5},{4,8},{5,9},{8,12},{9,13},{12,0},{13,1},{2,6},{3,7},{6... | collective-permute-start | bytes 294920 | tf_op jit(solution)/shard_map/ppermute | solution.py:728
  12.1 13.4 %collective-permute-start.3 = (bf16[384,128]{1,0:T(8,128)(2,1)S(1)}, bf16[384,128]{1,0:T(8,128)(2,1)S(1)}, u32[]{:S(2)}, u32[]{:S(2)}) collective-permute-start(bf16[384,128]{1,0:T(8,128)(2,1)S(1)} %get-tuple-element.34), channel_id=1, source_target_pairs={{0,5},{1,8},{4,9},{5,12},{8,13},{9,0},{12,1},{13,4},{2,7},{3,10},{... | collective-permute-start | bytes 294920 | tf_op jit(solution)/shard_map/ppermute | solution.py:728
  12.1 15.5 %collective-permute-start.4 = (bf16[384,128]{1,0:T(8,128)(2,1)S(1)}, bf16[384,128]{1,0:T(8,128)(2,1)S(1)}, u32[]{:S(2)}, u32[]{:S(2)}) collective-permute-start(bf16[384,128]{1,0:T(8,128)(2,1)S(1)} %get-tuple-element.35), channel_id=1, source_target_pairs={{0,8},{1,9},{4,12},{5,13},{8,0},{9,1},{12,4},{13,5},{2,10},{3,11},... | collective-permute-start | bytes 294920 | tf_op jit(solution)/shard_map/ppermute | solution.py:728
  13.5 14.1 %collective-permute-start.5 = (bf16[384,128]{1,0:T(8,128)(2,1)S(1)}, bf16[384,128]{1,0:T(8,128)(2,1)S(1)}, u32[]{:S(2)}, u32[]{:S(2)}) collective-permute-start(bf16[384,128]{1,0:T(8,128)(2,1)S(1)} %get-tuple-element.36), channel_id=1, source_target_pairs={{0,9},{1,12},{4,13},{5,0},{8,1},{9,4},{12,5},{13,8},{2,11},{3,14},... | collective-permute-start | bytes 294920 | tf_op jit(solution)/shard_map/ppermute | solution.py:728
  15.1 14.4 %collective-permute-start.6 = (bf16[384,128]{1,0:T(8,128)(2,1)S(1)}, bf16[384,128]{1,0:T(8,128)(2,1)S(1)}, u32[]{:S(2)}, u32[]{:S(2)}) collective-permute-start(bf16[384,128]{1,0:T(8,128)(2,1)S(1)} %get-tuple-element.37), channel_id=1, source_target_pairs={{0,12},{1,13},{4,0},{5,1},{8,4},{9,5},{12,8},{13,9},{2,14},{3,15},... | collective-permute-start | bytes 294920 | tf_op jit(solution)/shard_map/ppermute | solution.py:728
  16.3 13.4 %collective-permute-start.7 = (bf16[384,128]{1,0:T(8,128)(2,1)S(1)}, bf16[384,128]{1,0:T(8,128)(2,1)S(1)}, u32[]{:S(2)}, u32[]{:S(2)}) collective-permute-start(bf16[384,128]{1,0:T(8,128)(2,1)S(1)} %get-tuple-element.38), channel_id=1, source_target_pairs={{0,13},{1,0},{4,1},{5,4},{8,5},{9,8},{12,9},{13,12},{2,15},{3,2},{... | collective-permute-start | bytes 294920 | tf_op jit(solution)/shard_map/ppermute | solution.py:728
  37.3 4.5 %collective-permute-start.10 = (bf16[320,128]{1,0:T(8,128)(2,1)S(1)}, bf16[320,128]{1,0:T(8,128)(2,1)S(1)}, u32[]{:S(2)}, u32[]{:S(2)}) collective-permute-start(bf16[320,128]{1,0:T(8,128)(2,1)S(1)} %get-tuple-element.42), channel_id=1, source_target_pairs={{0,1},{1,4},{4,5},{5,8},{8,9},{9,12},{12,13},{13,0},{2,3},{3,6},{6... | collective-permute-start | bytes 245768 | tf_op jit(solution)/shard_map/ppermute | solution.py:728
  37.4 5.8 %collective-permute-start.11 = (bf16[320,128]{1,0:T(8,128)(2,1)S(1)}, bf16[320,128]{1,0:T(8,128)(2,1)S(1)}, u32[]{:S(2)}, u32[]{:S(2)}) collective-permute-start(bf16[320,128]{1,0:T(8,128)(2,1)S(1)} %get-tuple-element.43), channel_id=1, source_target_pairs={{0,4},{1,5},{4,8},{5,9},{8,12},{9,13},{12,0},{13,1},{2,6},{3,7},{6... | collective-permute-start | bytes 245768 | tf_op jit(solution)/shard_map/ppermute | solution.py:728
  38.1 11.3 %collective-permute-start.12 = (bf16[320,128]{1,0:T(8,128)(2,1)S(1)}, bf16[320,128]{1,0:T(8,128)(2,1)S(1)}, u32[]{:S(2)}, u32[]{:S(2)}) collective-permute-start(bf16[320,128]{1,0:T(8,128)(2,1)S(1)} %get-tuple-element.44), channel_id=1, source_target_pairs={{0,5},{1,8},{4,9},{5,12},{8,13},{9,0},{12,1},{13,4},{2,7},{3,10},{... | collective-permute-start | bytes 245768 | tf_op jit(solution)/shard_map/ppermute | solution.py:728
  39.1 12.1 %collective-permute-start.13 = (bf16[320,128]{1,0:T(8,128)(2,1)S(1)}, bf16[320,128]{1,0:T(8,128)(2,1)S(1)}, u32[]{:S(2)}, u32[]{:S(2)}) collective-permute-start(bf16[320,128]{1,0:T(8,128)(2,1)S(1)} %get-tuple-element.45), channel_id=1, source_target_pairs={{0,8},{1,9},{4,12},{5,13},{8,0},{9,1},{12,4},{13,5},{2,10},{3,11},... | collective-permute-start | bytes 245768 | tf_op jit(solution)/shard_map/ppermute | solution.py:728
  40.1 11.2 %collective-permute-start.14 = (bf16[320,128]{1,0:T(8,128)(2,1)S(1)}, bf16[320,128]{1,0:T(8,128)(2,1)S(1)}, u32[]{:S(2)}, u32[]{:S(2)}) collective-permute-start(bf16[320,128]{1,0:T(8,128)(2,1)S(1)} %get-tuple-element.46), channel_id=1, source_target_pairs={{0,9},{1,12},{4,13},{5,0},{8,1},{9,4},{12,5},{13,8},{2,11},{3,14},... | collective-permute-start | bytes 245768 | tf_op jit(solution)/shard_map/ppermute | solution.py:728
  41.8 11.9 %collective-permute-start.8 = (bf16[320,128]{1,0:T(8,128)(2,1)S(1)}, bf16[320,128]{1,0:T(8,128)(2,1)S(1)}, u32[]{:S(2)}, u32[]{:S(2)}) collective-permute-start(bf16[320,128]{1,0:T(8,128)(2,1)S(1)} %get-tuple-element.40), channel_id=1, source_target_pairs={{0,12},{1,13},{4,0},{5,1},{8,4},{9,5},{12,8},{13,9},{2,14},{3,15},... | collective-permute-start | bytes 245768 | tf_op jit(solution)/shard_map/ppermute | solution.py:728
  43.2 10.6 %collective-permute-start.9 = (bf16[320,128]{1,0:T(8,128)(2,1)S(1)}, bf16[320,128]{1,0:T(8,128)(2,1)S(1)}, u32[]{:S(2)}, u32[]{:S(2)}) collective-permute-start(bf16[320,128]{1,0:T(8,128)(2,1)S(1)} %get-tuple-element.41), channel_id=1, source_target_pairs={{0,13},{1,0},{4,1},{5,4},{8,5},{9,8},{12,9},{13,12},{2,15},{3,2},{... | collective-permute-start | bytes 245768 | tf_op jit(solution)/shard_map/ppermute | solution.py:728

commit v4 on v3

--- a/solution.py
+++ b/solution.py
@@ -713,11 +713,11 @@
 
 
 def first_order(count):
-    return tuple(range(count))
+    return (0, 2, 1) + tuple(range(3, count))
 
 
 def last_order(count):
-    return (0, count - 2, count - 1) + tuple(range(1, count - 2))
+    return (0, count - 2, count - 1, 2, 1) + tuple(range(3, count - 2))
 
 
 def spread_out(pieces, axes, order):

time: 56.1 us -> 55.1 us (0.982)
  the two profiles are of different devices: /device:TPU:9 before, /device:TPU:0 now
where the time goes in v4:
time: 55.1 us; the launch traced here: 54 us
  starting transfers between devices  25.4 us (46%)
  Pallas kernels  15.3 us (28%)
  waiting for transfers between devices  11.5 us (21%)
  local copies, waits for them, and re-layouts  1.14 us (2%)
  between operations  0.74 us (1%)
    ppermute x14, starting transfers between devices, spread_out(): received.append(lax.ppermute(pieces[slot], axes, pairs))  22.4 us
    pallas_call x5, Pallas kernels, call(): pl.pallas_call(kernel, out_shape=outs, in_specs=[place] * len(args), out_...  15.3 us
    ppermute x14, waiting for transfers between devices, spread_out(): received.append(lax.ppermute(pieces[slot], axes, pairs))  11.5 us
    ppermute x1, starting transfers between devices, by_columns(): halo = lax.ppermute(edge, 'sect', [(0, 1), (1, 0)])  3 us
    unnamed x14, local copies, waits for them, and re-layouts  1.13 us
  transfers between devices with their start and end apart: 15, of which 5 were waited for; matrix products, arithmetic and copies ran while one was open for 0% of the time, Pallas kernels for 4%

profile of v4, /device:TPU:0, one launch (start us, length us, event | category | flops | bytes accessed | tf_op | source)
XLA Modules:
  0.0 54.0 jit_solution(11739115410264849480)
XLA Ops:
  0.6 2.7 %shard_map.139 = (bf16[2784,128]{1,0:T(8,128)(2,1)}, bf16[192,128]{1,0:T(8,128)(2,1)}) custom-call(bf16[144,16,128]{2,1,0:T(8,128)(2,1)} %x_hbm.1, f32[32,4,128]{2,1,0:T(4,128)} %air_hbm.1, f32[32,4,128]{2,1,0:T(4,128)} %ocean_hbm.1, s32[4,128]{1,0:T(4,128)} %sea_hbm.1, f32[1,144]{1,0:T(1,128)} %bitcast.2, f32[1,144]{1,0:T(1,128)} %bitcast.3), custom_call_target="tpu_custom_call" | custom-call | bytes 4000000 | tf_op jit(solution)/shard_map/pallas_call | solution.py:751
  3.3 3.0 %collective-permute-start = (bf16[192,128]{1,0:T(8,128)(2,1)}, bf16[192,128]{1,0:T(8,128)(2,1)S(1)}, u32[]{:S(2)}, u32[]{:S(2)}) collective-permute-start(bf16[192,128]{1,0:T(8,128)(2,1)} %get-tuple-element.28), channel_id=1, source_target_pairs={{0,2},{2,0},{1,3},{3,1},{4,6},{6,4},{5,7},{7,5},{8,10},{10,8},{9,1... | collective-permute-start | bytes 147464 | tf_op jit(solution)/shard_map/ppermute | solution.py:774
  6.3 1.1 %copy-done.5 = bf16[2784,128]{1,0:T(8,128)(2,1)S(1)} copy-done((bf16[2784,128]{1,0:T(8,128)(2,1)S(1)}, bf16[2784,128]{1,0:T(8,128)(2,1)}, u32[]{:S(2)}) %copy-start.5) | copy-done | bytes 712728
  7.4 0.0 copy-start.4
  7.4 2.4 %shard_map.140 = (bf16[8,384,128]{2,1,0:T(8,128)(2,1)S(1)}, f32[144,128]{1,0:T(8,128)S(1)}, f32[144,128]{1,0:T(8,128)S(1)}, bf16[144,128]{1,0:T(8,128)(2,1)S(1)}) custom-call(bf16[2784,128]{1,0:T(8,128)(2,1)S(1)} %copy-done.5), custom_call_target="tpu_custom_call" | custom-call | flops 2000000000 | bytes 4000000 | tf_op jit(solution)/shard_map/pallas_call | solution.py:751
  9.8 0.0 collective-permute-done.halo_ref
  9.8 0.5 shard_map.141
  10.4 0.0 copy-start.1
  10.4 1.6 %collective-permute-start.1 = (bf16[384,128]{1,0:T(8,128)(2,1)S(1)}, bf16[384,128]{1,0:T(8,128)(2,1)S(1)}, u32[]{:S(2)}, u32[]{:S(2)}) collective-permute-start(bf16[384,128]{1,0:T(8,128)(2,1)S(1)} %get-tuple-element.32), channel_id=1, source_target_pairs={{0,4},{1,5},{4,8},{5,9},{8,12},{9,13},{12,0},{13,1},{2,6},{3,7},{6... | collective-permute-start | bytes 294920 | tf_op jit(solution)/shard_map/ppermute | solution.py:728
  12.0 0.0 collective-permute-start.2
  12.0 2.9 %collective-permute-start.3 = (bf16[384,128]{1,0:T(8,128)(2,1)S(1)}, bf16[384,128]{1,0:T(8,128)(2,1)S(1)}, u32[]{:S(2)}, u32[]{:S(2)}) collective-permute-start(bf16[384,128]{1,0:T(8,128)(2,1)S(1)} %get-tuple-element.34), channel_id=1, source_target_pairs={{0,5},{1,8},{4,9},{5,12},{8,13},{9,0},{12,1},{13,4},{2,7},{3,10},{... | collective-permute-start | bytes 294920 | tf_op jit(solution)/shard_map/ppermute | solution.py:728
  14.9 1.2 %collective-permute-start.4 = (bf16[384,128]{1,0:T(8,128)(2,1)S(1)}, bf16[384,128]{1,0:T(8,128)(2,1)S(1)}, u32[]{:S(2)}, u32[]{:S(2)}) collective-permute-start(bf16[384,128]{1,0:T(8,128)(2,1)S(1)} %get-tuple-element.35), channel_id=1, source_target_pairs={{0,8},{1,9},{4,12},{5,13},{8,0},{9,1},{12,4},{13,5},{2,10},{3,11},... | collective-permute-start | bytes 294920 | tf_op jit(solution)/shard_map/ppermute | solution.py:728
  16.1 0.9 %collective-permute-start.5 = (bf16[384,128]{1,0:T(8,128)(2,1)S(1)}, bf16[384,128]{1,0:T(8,128)(2,1)S(1)}, u32[]{:S(2)}, u32[]{:S(2)}) collective-permute-start(bf16[384,128]{1,0:T(8,128)(2,1)S(1)} %get-tuple-element.36), channel_id=1, source_target_pairs={{0,9},{1,12},{4,13},{5,0},{8,1},{9,4},{12,5},{13,8},{2,11},{3,14},... | collective-permute-start | bytes 294920 | tf_op jit(solution)/shard_map/ppermute | solution.py:728
  17.0 0.0 collective-permute-done.1.refs_1_
  17.0 2.3 %collective-permute-start.6 = (bf16[384,128]{1,0:T(8,128)(2,1)S(1)}, bf16[384,128]{1,0:T(8,128)(2,1)S(1)}, u32[]{:S(2)}, u32[]{:S(2)}) collective-permute-start(bf16[384,128]{1,0:T(8,128)(2,1)S(1)} %get-tuple-element.37), channel_id=1, source_target_pairs={{0,12},{1,13},{4,0},{5,1},{8,4},{9,5},{12,8},{13,9},{2,14},{3,15},... | collective-permute-start | bytes 294920 | tf_op jit(solution)/shard_map/ppermute | solution.py:728
  19.4 0.7 %collective-permute-start.7 = (bf16[384,128]{1,0:T(8,128)(2,1)S(1)}, bf16[384,128]{1,0:T(8,128)(2,1)S(1)}, u32[]{:S(2)}, u32[]{:S(2)}) collective-permute-start(bf16[384,128]{1,0:T(8,128)(2,1)S(1)} %get-tuple-element.38), channel_id=1, source_target_pairs={{0,13},{1,0},{4,1},{5,4},{8,5},{9,8},{12,9},{13,12},{2,15},{3,2},{... | collective-permute-start | bytes 294920 | tf_op jit(solution)/shard_map/ppermute | solution.py:728
  20.1 5.2 %collective-permute-done.3.refs_3_ = bf16[384,128]{1,0:T(8,128)(2,1)S(1)} collective-permute-done((bf16[384,128]{1,0:T(8,128)(2,1)S(1)}, bf16[384,128]{1,0:T(8,128)(2,1)S(1)}, u32[]{:S(2)}, u32[]{:S(2)}) %collective-permute-start.3) | collective-permute-done | bytes 98336 | tf_op jit(solution)/shard_map/ppermute | solution.py:728
  25.3 0.2 collective-permute-done.4.refs_4_
  25.5 0.0 collective-permute-done.5.refs_5_
  25.5 0.0 collective-permute-done.6.refs_6_
  25.5 7.6 %shard_map.142 = (bf16[320,128]{1,0:T(8,128)(2,1)S(1)}, bf16[320,128]{1,0:T(8,128)(2,1)S(1)}, bf16[320,128]{1,0:T(8,128)(2,1)S(1)}, bf16[320,128]{1,0:T(8,128)(2...) custom-call(bf16[1152,1152]{1,0:T(8,128)(2,1)S(1)} %copy-done, ...), custom_call_target="tpu_custom_call" | custom-call | bytes 4000000 | tf_op jit(solution)/shard_map/pallas_call | solution.py:751
  33.2 5.0 %collective-permute-start.10 = (bf16[320,128]{1,0:T(8,128)(2,1)S(1)}, bf16[320,128]{1,0:T(8,128)(2,1)S(1)}, u32[]{:S(2)}, u32[]{:S(2)}) collective-permute-start(bf16[320,128]{1,0:T(8,128)(2,1)S(1)} %get-tuple-element.42), channel_id=1, source_target_pairs={{0,4},{1,5},{4,8},{5,9},{8,12},{9,13},{12,0},{13,1},{2,6},{3,7},{6... | collective-permute-start | bytes 245768 | tf_op jit(solution)/shard_map/ppermute | solution.py:728
  38.2 1.3 %collective-permute-start.11 = (bf16[320,128]{1,0:T(8,128)(2,1)S(1)}, bf16[320,128]{1,0:T(8,128)(2,1)S(1)}, u32[]{:S(2)}, u32[]{:S(2)}) collective-permute-start(bf16[320,128]{1,0:T(8,128)(2,1)S(1)} %get-tuple-element.43), channel_id=1, source_target_pairs={{0,1},{1,4},{4,5},{5,8},{8,9},{9,12},{12,13},{13,0},{2,3},{3,6},{6... | collective-permute-start | bytes 245768 | tf_op jit(solution)/shard_map/ppermute | solution.py:728
  39.5 0.7 %collective-permute-start.12 = (bf16[320,128]{1,0:T(8,128)(2,1)S(1)}, bf16[320,128]{1,0:T(8,128)(2,1)S(1)}, u32[]{:S(2)}, u32[]{:S(2)}) collective-permute-start(bf16[320,128]{1,0:T(8,128)(2,1)S(1)} %get-tuple-element.44), channel_id=1, source_target_pairs={{0,5},{1,8},{4,9},{5,12},{8,13},{9,0},{12,1},{13,4},{2,7},{3,10},{... | collective-permute-start | bytes 245768 | tf_op jit(solution)/shard_map/ppermute | solution.py:728
  40.2 2.1 %collective-permute-start.13 = (bf16[320,128]{1,0:T(8,128)(2,1)S(1)}, bf16[320,128]{1,0:T(8,128)(2,1)S(1)}, u32[]{:S(2)}, u32[]{:S(2)}) collective-permute-start(bf16[320,128]{1,0:T(8,128)(2,1)S(1)} %get-tuple-element.45), channel_id=1, source_target_pairs={{0,8},{1,9},{4,12},{5,13},{8,0},{9,1},{12,4},{13,5},{2,10},{3,11},... | collective-permute-start | bytes 245768 | tf_op jit(solution)/shard_map/ppermute | solution.py:728
  42.3 1.2 %collective-permute-start.14 = (bf16[320,128]{1,0:T(8,128)(2,1)S(1)}, bf16[320,128]{1,0:T(8,128)(2,1)S(1)}, u32[]{:S(2)}, u32[]{:S(2)}) collective-permute-start(bf16[320,128]{1,0:T(8,128)(2,1)S(1)} %get-tuple-element.46), channel_id=1, source_target_pairs={{0,9},{1,12},{4,13},{5,0},{8,1},{9,4},{12,5},{13,8},{2,11},{3,14},... | collective-permute-start | bytes 245768 | tf_op jit(solution)/shard_map/ppermute | solution.py:728
  43.5 1.1 %collective-permute-start.8 = (bf16[320,128]{1,0:T(8,128)(2,1)S(1)}, bf16[320,128]{1,0:T(8,128)(2,1)S(1)}, u32[]{:S(2)}, u32[]{:S(2)}) collective-permute-start(bf16[320,128]{1,0:T(8,128)(2,1)S(1)} %get-tuple-element.40), channel_id=1, source_target_pairs={{0,12},{1,13},{4,0},{5,1},{8,4},{9,5},{12,8},{13,9},{2,14},{3,15},... | collective-permute-start | bytes 245768 | tf_op jit(solution)/shard_map/ppermute | solution.py:728
  44.5 1.4 %collective-permute-start.9 = (bf16[320,128]{1,0:T(8,128)(2,1)S(1)}, bf16[320,128]{1,0:T(8,128)(2,1)S(1)}, u32[]{:S(2)}, u32[]{:S(2)}) collective-permute-start(bf16[320,128]{1,0:T(8,128)(2,1)S(1)} %get-tuple-element.41), channel_id=1, source_target_pairs={{0,13},{1,0},{4,1},{5,4},{8,5},{9,8},{12,9},{13,12},{2,15},{3,2},{... | collective-permute-start | bytes 245768 | tf_op jit(solution)/shard_map/ppermute | solution.py:728
  45.9 4.0 %collective-permute-done.12.refs_5_ = bf16[320,128]{1,0:T(8,128)(2,1)S(1)} collective-permute-done((bf16[320,128]{1,0:T(8,128)(2,1)S(1)}, bf16[320,128]{1,0:T(8,128)(2,1)S(1)}, u32[]{:S(2)}, u32[]{:S(2)}) %collective-permute-start.12) | collective-permute-done | bytes 81952 | tf_op jit(solution)/shard_map/ppermute | solution.py:728
  49.9 0.3 collective-permute-done.13.refs_6_
  50.2 1.7 %collective-permute-done.8.refs_1_ = bf16[320,128]{1,0:T(8,128)(2,1)S(1)} collective-permute-done((bf16[320,128]{1,0:T(8,128)(2,1)S(1)}, bf16[320,128]{1,0:T(8,128)(2,1)S(1)}, u32[]{:S(2)}, u32[]{:S(2)}) %collective-permute-start.8) | collective-permute-done | bytes 81952 | tf_op jit(solution)/shard_map/ppermute | solution.py:728
  51.9 2.1 %shard_map.143 = (bf16[144,16,128]{2,1,0:T(8,128)(2,1)}, f32[32,4,128]{2,1,0:T(4,128)}, f32[32,4,128]{2,1,0:T(4,128)}) custom-call(bf16[1024,1024]{1,0:T(8,128)(2,1)S(1)} %copy-done.1, bf16[320,128]{1,0:T(8,128)(2,1)S(1)} %get-tuple-element.39.refs_0_, bf16[320,128]{1,0:T(8,128)(2,1)S(1)} %collective-permute-done.8.refs_1_, ...), custom_call_target="tpu_custom_call" | custom-call | bytes 4000000 | tf_op jit(solution)/shard_map/pallas_call | solution.py:751
  (18 shorter events, 0.0 us)
Async XLA Ops:
  3.3 6.5 %collective-permute-start = (bf16[192,128]{1,0:T(8,128)(2,1)}, bf16[192,128]{1,0:T(8,128)(2,1)S(1)}, u32[]{:S(2)}, u32[]{:S(2)}) collective-permute-start(bf16[192,128]{1,0:T(8,128)(2,1)} %get-tuple-element.28), channel_id=1, source_target_pairs={{0,2},{2,0},{1,3},{3,1},{4,6},{6,4},{5,7},{7,5},{8,10},{10,8},{9,1... | collective-permute-start | bytes 147464 | tf_op jit(solution)/shard_map/ppermute | solution.py:774
  6.3 1.1 %copy-start.5 = (bf16[2784,128]{1,0:T(8,128)(2,1)S(1)}, bf16[2784,128]{1,0:T(8,128)(2,1)}, u32[]{:S(2)}) copy-start(bf16[2784,128]{1,0:T(8,128)(2,1)} %get-tuple-element.25.all_ref) | copy-start | bytes 2138116
  7.4 12.6 %copy-start.6 = (f32[1152]{0:T(1024)S(1)}, f32[1152]{0:T(1024)}, u32[]{:S(2)}) copy-start(f32[1152]{0:T(1024)} %param.15) | copy-start | bytes 13828
  7.4 18.1 %copy-start = (bf16[1152,1152]{1,0:T(8,128)(2,1)S(1)}, bf16[1152,1152]{1,0:T(8,128)(2,1)}, u32[]{:S(2)}) copy-start(bf16[1152,1152]{1,0:T(8,128)(2,1)} %quartet_ref.1) | copy-start | bytes 7962628
  7.4 18.1 %copy-start.2 = (bf16[384,1024]{1,0:T(8,128)(2,1)S(1)}, bf16[384,1024]{1,0:T(8,128)(2,1)}, u32[]{:S(2)}) copy-start(bf16[384,1024]{1,0:T(8,128)(2,1)} %constant.7.clone.beside_ref) | copy-start | bytes 2359300
  7.4 18.1 %copy-start.3 = (bf16[512,384]{1,0:T(8,128)(2,1)S(1)}, bf16[512,384]{1,0:T(8,128)(2,1)}, u32[]{:S(2)}) copy-start(bf16[512,384]{1,0:T(8,128)(2,1)} %constant.8.clone.lateral_ref) | copy-start | bytes 1179652
  7.4 18.1 %copy-start.4 = (bf16[128,1152]{1,0:T(8,128)(2,1)S(1)}, bf16[128,1152]{1,0:T(8,128)(2,1)}, u32[]{:S(2)}) copy-start(bf16[128,1152]{1,0:T(8,128)(2,1)} %coupler_ref.1) | copy-start | bytes 884740
  10.4 41.6 %copy-start.1 = (bf16[1024,1024]{1,0:T(8,128)(2,1)S(1)}, bf16[1024,1024]{1,0:T(8,128)(2,1)}, u32[]{:S(2)}) copy-start(bf16[1024,1024]{1,0:T(8,128)(2,1)} %constant.6.clone.swap_ref) | copy-start | bytes 6291460
  10.4 6.6 %collective-permute-start.1 = (bf16[384,128]{1,0:T(8,128)(2,1)S(1)}, bf16[384,128]{1,0:T(8,128)(2,1)S(1)}, u32[]{:S(2)}, u32[]{:S(2)}) collective-permute-start(bf16[384,128]{1,0:T(8,128)(2,1)S(1)} %get-tuple-element.32), channel_id=1, source_target_pairs={{0,4},{1,5},{4,8},{5,9},{8,12},{9,13},{12,0},{13,1},{2,6},{3,7},{6... | collective-permute-start | bytes 294920 | tf_op jit(solution)/shard_map/ppermute | solution.py:728
  12.0 7.4 %collective-permute-start.2 = (bf16[384,128]{1,0:T(8,128)(2,1)S(1)}, bf16[384,128]{1,0:T(8,128)(2,1)S(1)}, u32[]{:S(2)}, u32[]{:S(2)}) collective-permute-start(bf16[384,128]{1,0:T(8,128)(2,1)S(1)} %get-tuple-element.33), channel_id=1, source_target_pairs={{0,1},{1,4},{4,5},{5,8},{8,9},{9,12},{12,13},{13,0},{2,3},{3,6},{6... | collective-permute-start | bytes 294920 | tf_op jit(solution)/shard_map/ppermute | solution.py:728
  12.0 13.3 %collective-permute-start.3 = (bf16[384,128]{1,0:T(8,128)(2,1)S(1)}, bf16[384,128]{1,0:T(8,128)(2,1)S(1)}, u32[]{:S(2)}, u32[]{:S(2)}) collective-permute-start(bf16[384,128]{1,0:T(8,128)(2,1)S(1)} %get-tuple-element.34), channel_id=1, source_target_pairs={{0,5},{1,8},{4,9},{5,12},{8,13},{9,0},{12,1},{13,4},{2,7},{3,10},{... | collective-permute-start | bytes 294920 | tf_op jit(solution)/shard_map/ppermute | solution.py:728
  14.9 10.6 %collective-permute-start.4 = (bf16[384,128]{1,0:T(8,128)(2,1)S(1)}, bf16[384,128]{1,0:T(8,128)(2,1)S(1)}, u32[]{:S(2)}, u32[]{:S(2)}) collective-permute-start(bf16[384,128]{1,0:T(8,128)(2,1)S(1)} %get-tuple-element.35), channel_id=1, source_target_pairs={{0,8},{1,9},{4,12},{5,13},{8,0},{9,1},{12,4},{13,5},{2,10},{3,11},... | collective-permute-start | bytes 294920 | tf_op jit(solution)/shard_map/ppermute | solution.py:728
  16.1 9.4 %collective-permute-start.5 = (bf16[384,128]{1,0:T(8,128)(2,1)S(1)}, bf16[384,128]{1,0:T(8,128)(2,1)S(1)}, u32[]{:S(2)}, u32[]{:S(2)}) collective-permute-start(bf16[384,128]{1,0:T(8,128)(2,1)S(1)} %get-tuple-element.36), channel_id=1, source_target_pairs={{0,9},{1,12},{4,13},{5,0},{8,1},{9,4},{12,5},{13,8},{2,11},{3,14},... | collective-permute-start | bytes 294920 | tf_op jit(solution)/shard_map/ppermute | solution.py:728
  17.0 8.5 %collective-permute-start.6 = (bf16[384,128]{1,0:T(8,128)(2,1)S(1)}, bf16[384,128]{1,0:T(8,128)(2,1)S(1)}, u32[]{:S(2)}, u32[]{:S(2)}) collective-permute-start(bf16[384,128]{1,0:T(8,128)(2,1)S(1)} %get-tuple-element.37), channel_id=1, source_target_pairs={{0,12},{1,13},{4,0},{5,1},{8,4},{9,5},{12,8},{13,9},{2,14},{3,15},... | collective-permute-start | bytes 294920 | tf_op jit(solution)/shard_map/ppermute | solution.py:728
  19.4 6.1 %collective-permute-start.7 = (bf16[384,128]{1,0:T(8,128)(2,1)S(1)}, bf16[384,128]{1,0:T(8,128)(2,1)S(1)}, u32[]{:S(2)}, u32[]{:S(2)}) collective-permute-start(bf16[384,128]{1,0:T(8,128)(2,1)S(1)} %get-tuple-element.38), channel_id=1, source_target_pairs={{0,13},{1,0},{4,1},{5,4},{8,5},{9,8},{12,9},{13,12},{2,15},{3,2},{... | collective-permute-start | bytes 294920 | tf_op jit(solution)/shard_map/ppermute | solution.py:728
  33.2 10.3 %collective-permute-start.10 = (bf16[320,128]{1,0:T(8,128)(2,1)S(1)}, bf16[320,128]{1,0:T(8,128)(2,1)S(1)}, u32[]{:S(2)}, u32[]{:S(2)}) collective-permute-start(bf16[320,128]{1,0:T(8,128)(2,1)S(1)} %get-tuple-element.42), channel_id=1, source_target_pairs={{0,4},{1,5},{4,8},{5,9},{8,12},{9,13},{12,0},{13,1},{2,6},{3,7},{6... | collective-permute-start | bytes 245768 | tf_op jit(solution)/shard_map/ppermute | solution.py:728
  38.2 6.3 %collective-permute-start.11 = (bf16[320,128]{1,0:T(8,128)(2,1)S(1)}, bf16[320,128]{1,0:T(8,128)(2,1)S(1)}, u32[]{:S(2)}, u32[]{:S(2)}) collective-permute-start(bf16[320,128]{1,0:T(8,128)(2,1)S(1)} %get-tuple-element.43), channel_id=1, source_target_pairs={{0,1},{1,4},{4,5},{5,8},{8,9},{9,12},{12,13},{13,0},{2,3},{3,6},{6... | collective-permute-start | bytes 245768 | tf_op jit(solution)/shard_map/ppermute | solution.py:728
  39.5 10.4 %collective-permute-start.12 = (bf16[320,128]{1,0:T(8,128)(2,1)S(1)}, bf16[320,128]{1,0:T(8,128)(2,1)S(1)}, u32[]{:S(2)}, u32[]{:S(2)}) collective-permute-start(bf16[320,128]{1,0:T(8,128)(2,1)S(1)} %get-tuple-element.44), channel_id=1, source_target_pairs={{0,5},{1,8},{4,9},{5,12},{8,13},{9,0},{12,1},{13,4},{2,7},{3,10},{... | collective-permute-start | bytes 245768 | tf_op jit(solution)/shard_map/ppermute | solution.py:728
  40.2 10.0 %collective-permute-start.13 = (bf16[320,128]{1,0:T(8,128)(2,1)S(1)}, bf16[320,128]{1,0:T(8,128)(2,1)S(1)}, u32[]{:S(2)}, u32[]{:S(2)}) collective-permute-start(bf16[320,128]{1,0:T(8,128)(2,1)S(1)} %get-tuple-element.45), channel_id=1, source_target_pairs={{0,8},{1,9},{4,12},{5,13},{8,0},{9,1},{12,4},{13,5},{2,10},{3,11},... | collective-permute-start | bytes 245768 | tf_op jit(solution)/shard_map/ppermute | solution.py:728
  42.3 7.9 %collective-permute-start.14 = (bf16[320,128]{1,0:T(8,128)(2,1)S(1)}, bf16[320,128]{1,0:T(8,128)(2,1)S(1)}, u32[]{:S(2)}, u32[]{:S(2)}) collective-permute-start(bf16[320,128]{1,0:T(8,128)(2,1)S(1)} %get-tuple-element.46), channel_id=1, source_target_pairs={{0,9},{1,12},{4,13},{5,0},{8,1},{9,4},{12,5},{13,8},{2,11},{3,14},... | collective-permute-start | bytes 245768 | tf_op jit(solution)/shard_map/ppermute | solution.py:728
  43.5 8.4 %collective-permute-start.8 = (bf16[320,128]{1,0:T(8,128)(2,1)S(1)}, bf16[320,128]{1,0:T(8,128)(2,1)S(1)}, u32[]{:S(2)}, u32[]{:S(2)}) collective-permute-start(bf16[320,128]{1,0:T(8,128)(2,1)S(1)} %get-tuple-element.40), channel_id=1, source_target_pairs={{0,12},{1,13},{4,0},{5,1},{8,4},{9,5},{12,8},{13,9},{2,14},{3,15},... | collective-permute-start | bytes 245768 | tf_op jit(solution)/shard_map/ppermute | solution.py:728
  44.5 7.4 %collective-permute-start.9 = (bf16[320,128]{1,0:T(8,128)(2,1)S(1)}, bf16[320,128]{1,0:T(8,128)(2,1)S(1)}, u32[]{:S(2)}, u32[]{:S(2)}) collective-permute-start(bf16[320,128]{1,0:T(8,128)(2,1)S(1)} %get-tuple-element.41), channel_id=1, source_target_pairs={{0,13},{1,0},{4,1},{5,4},{8,5},{9,8},{12,9},{13,12},{2,15},{3,2},{... | collective-permute-start | bytes 245768 | tf_op jit(solution)/shard_map/ppermute | solution.py:728
